TPU v7x, 512 devices: a whole 4x4x16 slice. The times are simulated.
512 devices in a mesh: row: 16 (over x_lo, y, core), col: 32 (over x_hi, z).
Axes of the slice: x: 4 (x_hi: 2, x_lo: 2; x = x_hi * 2 + x_lo), y: 4, z: 16, core: 2. Of those that a mesh axis runs over, the one named last changes fastest.
Arguments:
- matrix: float32 [8, 16, 128, 4, 32, 128], P(None, 'row', None, None, 'col'), may hold values from -8.5 to 8.5
- vectors: float32 [2, 8, 16, 128, 96], P(None, None, 'row', 'col'), may hold values from -0.046875 to 0.046875
- factors: float32 [2, 96, 96], replicated, may hold values from -0.30618622 to 1.6, as said below
Outputs:
- updated: float32 [8, 16, 128, 4, 32, 128], P(None, 'row', None, None, 'col')
Inputs may be any that keep to these rules, and one draw needn't show every extreme that they name: Each factors[k] is upper triangular with a positive diagonal.
All inputs are finite; a program needn't handle non-finite values.
Results may differ from a plain program's by a relative error of at most 0.0001.
Values sent between devices are 32-bit elements; how exact they have to be, the bound alone decides.
No kernel may reach another device: no remote copies, remote signals or barrier semaphores. Data moves between devices by JAX's collectives and lax.ppermute only.
A program may use at most 64 MiB of HBM per device.

v0:
```python
import jax
import jax.numpy as jnp
from jax import lax
from jax.sharding import Mesh
from jax.sharding import PartitionSpec as P

COL = ("col_0", "col_1")


def in_order(tiles, dim):
    tiles = jnp.moveaxis(tiles, 0, dim)
    shape = tiles.shape
    return tiles.reshape(*shape[:dim], shape[dim] * shape[dim + 1], *shape[dim + 2 :])


def stacked_from(array, axes, order):
    tiles = array
    for k in order:
        tiles = lax.all_gather(tiles, axes[k])
    done = order[::-1]
    back = [done.index(k) for k in range(len(axes))]
    tiles = tiles.transpose(*back, *range(len(axes), tiles.ndim))
    return tiles.reshape(-1, *array.shape)


def whole_of(array, axes, order, dim):
    return in_order(stacked_from(array, axes, order), dim)


def from_root(array, axis, root):
    return lax.dynamic_index_in_dim(lax.all_gather(array, axis), root, 0, keepdims=False)


def rows_for(lines, length):
    spare = -len(lines) % length
    return jnp.pad(lines, [(0, spare)] + [(0, 0)] * (lines.ndim - 1))


def reduced_to_own(tiles, axes, order):
    shape = [lax.axis_size(a) for a in axes]
    tiles = tiles.reshape(*shape, *tiles.shape[1:])
    tiles = tiles.transpose(*order, *range(len(axes), tiles.ndim))
    tiles = tiles.reshape(-1, *tiles.shape[len(axes) :])
    for k in order:
        tiles = lax.psum_scatter(tiles, axes[k], scatter_dimension=0, tiled=True)
    return tiles[0]


def sum_in_two_steps(array, axes, order):
    length, lines = (lax.axis_size(axes), array.reshape(-1, *array.shape[1:][-1:]))
    tiles = rows_for(lines, length).reshape(length, -1, *lines.shape[1:])
    own = reduced_to_own(tiles, axes, order)
    whole = stacked_from(own, axes, order[::-1]).reshape(-1, *lines.shape[1:])
    return whole[: len(lines)].reshape(array.shape)


def sent_to_all(array, axis):
    copies = jnp.broadcast_to(array, (lax.axis_size(axis), *array.shape))
    return lax.all_to_all(copies, axis, split_axis=0, concat_axis=0, tiled=True)


def of_everyone(array, axis):
    everything = sent_to_all(array, axis)
    return jnp.sum(everything, axis=0)


def product(matrix_a, matrix_b):
    return jnp.dot(
        matrix_a, matrix_b, precision=lax.Precision.HIGHEST, preferred_element_type=jnp.float32
    )


def contract(matrix_a, matrix_b):
    return lax.dot_general(
        matrix_a,
        matrix_b,
        (((0,), (0,)), ((), ())),
        precision=lax.Precision.HIGHEST,
        preferred_element_type=jnp.float32,
    )


def select_cols(rows, col_tiles, stride, parity):
    width = rows.shape[-1]
    tile_size = rows.shape[-2] // (col_tiles * stride)
    shaped = rows.reshape(rows.shape[:-2] + (col_tiles, stride, tile_size, width))
    axis_at = len(rows.shape) - 1
    picked = lax.dynamic_index_in_dim(shaped, parity, axis_at, keepdims=False)
    return picked.reshape(rows.shape[:-2] + (col_tiles * tile_size, width))


def rank_update(blocks, rows_left, update_rows, update_cols, cols_right):
    left_side = jnp.concatenate([rows_left, update_rows], axis=1)
    right_side = jnp.concatenate([update_cols, cols_right], axis=1)
    return blocks - lax.dot_general(
        left_side,
        right_side,
        (((1,), (1,)), ((), ())),
        precision=lax.Precision.HIGHEST,
        preferred_element_type=jnp.float32,
    )


def shards(matrix, vectors, factors):
    row_tiles, tile_size, col_tiles = (matrix.shape[0], matrix.shape[2], matrix.shape[3])
    panel_count, width = (factors.shape[0], factors.shape[1])
    n_rows = lax.axis_size("row")
    n_cols = lax.axis_size(COL)
    stride = n_cols // n_rows
    col_index = lax.axis_index(COL)
    source = col_index % n_rows
    parity = col_index // n_rows
    blocks = matrix.reshape(row_tiles * tile_size, col_tiles * tile_size)
    gathered = whole_of(vectors, COL, (0, 1), 3)
    basis_rows = gathered.reshape(panel_count, row_tiles * tile_size, width)
    basis_cols = from_root(select_cols(basis_rows, col_tiles, stride, parity), "row", source)
    rows_all = jnp.concatenate([basis_rows[0], basis_rows[1]], axis=1)
    cols_all = jnp.concatenate([basis_cols[0], basis_cols[1]], axis=1)
    image_all = sum_in_two_steps(product(blocks, cols_all), COL, (1, 0))
    gram_all = of_everyone(
        contract(rows_all, jnp.concatenate([rows_all, image_all], axis=1)), "row"
    )
    first_gram = gram_all[:width, 2 * width : 3 * width]
    basis_gram = gram_all[:width, width : 2 * width]
    image_gram = gram_all[width : 2 * width, 2 * width : 3 * width].T
    last_gram = gram_all[width : 2 * width, 3 * width :]
    factor_one = factors[0]
    factor_two = factors[1]
    shift_one = 0.5 * product(factor_one.T, product(first_gram, factor_one))
    crossed = product(factor_one.T, image_gram) - product(shift_one.T, basis_gram)
    secondary = last_gram - product(basis_gram.T, crossed) - product(crossed.T, basis_gram)
    shift_two = 0.5 * product(factor_two.T, product(secondary, factor_two))
    basis_one = basis_rows[0]
    update_one = product(image_all[:, :width], factor_one) - product(basis_one, shift_one)
    moved_two = image_all[:, width:] - product(basis_one, crossed) - product(update_one, basis_gram)
    update_two = product(moved_two, factor_two) - product(basis_rows[1], shift_two)
    update_rows = jnp.concatenate([update_one, update_two], axis=1)
    update_cols = from_root(select_cols(update_rows, col_tiles, stride, parity), "row", source)
    blocks = rank_update(blocks, rows_all, update_rows, update_cols, cols_all)
    return blocks.reshape(matrix.shape)


def solution(mesh):
    finer = Mesh(mesh.devices.reshape(mesh.shape["row"], 2, 16), ("row", "col_0", "col_1"))
    placed = (P(None, "row", None, None, COL, None), P(None, None, "row", COL, None), P())
    return jax.shard_map(
        shards,
        mesh=finer,
        in_specs=placed,
        out_specs=P(None, "row", None, None, COL, None),
        check_vma=False,
    )
```

profile of v0, /device:TPU:1, one launch (start us, length us, event | category | flops | bytes accessed | tf_op | source)
XLA Modules:
  0.0 407.8 jit_solution(6878309139434328542)
XLA Ops:
  7.3 5.5 %all-gather = f32[4,8,1,4,96]{4,1,3,2,0:T(8,128)S(1)} all-gather(f32[2,8,1,4,96]{4,1,3,2,0:T(8,128)S(1)} %copy.51), channel_id=2, replica_groups=mesh['row'=16,'col_0'=2,'col_1'=16] {'col_0'}, dimensions={0}, use_global_device_ids=true | all-gather | bytes 73728 | tf_op jit(solution)/shard_map/all_gather | solution.py:19
  12.8 35.7 %all-gather.1 = f32[32,2,8,1,4,96]{5,2,4,3,1,0:T(8,128)S(1)} all-gather(f32[2,2,8,1,4,96]{5,2,4,3,1,0:T(8,128)S(1)} %bitcast.106), channel_id=3, replica_groups=mesh['row'=16,'col_0'=2,'col_1'=16] {'col_1'}, dimensions={0}, use_global_device_ids=true | all-gather | bytes 835584 | tf_op jit(solution)/shard_map/all_gather | solution.py:19
  49.7 2.0 copy.55
  51.7 54.3 %all-gather.6.cloned.1.call-done = f32[16,2,512,96]{2,3,1,0:T(8,128)} async-done(((f32[1,2,512,96]{2,3,1,0:T(8,128)}), f32[16,2,512,96]{2,3,1,0:T(8,128)}) %all-gather.6.cloned.1.call-update) | async-done | bytes 6291472 | tf_op jit(solution)/shard_map/all_gather | solution.py:31
  106.0 1.0 dynamic-slice_bitcast_fusion.2
  107.8 3.2 fusion.16
  111.0 1.5 copy.56
  112.4 1.0 copy.57
  113.5 60.8 %reduce-scatter.3.cloned.1.call-done = f32[2,32,192]{2,1,0:T(8,128)} async-done(((f32[32,32,192]{2,1,0:T(8,128)}), f32[2,32,192]{2,1,0:T(8,128)}) %reduce-scatter.3.cloned.1.call-update) | async-done | bytes 49168 | tf_op jit(solution)/shard_map/reduce_scatter | solution.py:45
  174.4 32.1 %reduce-scatter.5.cloned.1.call-done = f32[1,32,192]{2,1,0:T(8,128)} async-done(((f32[2,32,192]{2,1,0:T(8,128)}), f32[1,32,192]{2,1,0:T(8,128)}) %reduce-scatter.5.cloned.1.call-update) | async-done | bytes 24592 | tf_op jit(solution)/shard_map/reduce_scatter | solution.py:45
  206.5 5.1 %all_gather.32 = f32[2,32,192]{2,1,0:T(8,128)S(1)} all-gather(f32[1,32,192]{2,1,0:T(8,128)} %reduce-scatter.5.cloned.1.call-done), channel_id=1, replica_groups=mesh['row'=16,'col_0'=2,'col_1'=16] {'col_0'}, dimensions={0}, use_global_device_ids=true | all-gather | bytes 73728 | tf_op jit(solution)/shard_map/all_gather | solution.py:19
  211.7 31.0 %all-gather.2 = f32[32,32,192]{2,1,0:T(8,128)S(1)} all-gather(f32[2,32,192]{2,1,0:T(8,128)S(1)} %all_gather.32), channel_id=4, replica_groups=mesh['row'=16,'col_0'=2,'col_1'=16] {'col_1'}, dimensions={0}, use_global_device_ids=true | all-gather | bytes 835584 | tf_op jit(solution)/shard_map/all_gather | solution.py:19
  242.7 2.9 fusion.3
  245.7 2.6 broadcast_in_dim.3
  248.3 13.1 %all-to-all-start = ((f32[16,192,384]{2,1,0:T(8,128)}), f32[16,192,384]{2,1,0:T(8,128)}, u32[]{:S(2)}, u32[]{:S(2)}) async-start(f32[16,192,384]{2,1,0:T(8,128)} %broadcast_in_dim.3), calls=%async_computation.2 | async-start | bytes 9437184 | tf_op jit(solution)/shard_map/all_to_all | solution.py:59
  262.7 61.2 %all-to-all-done = f32[16,192,384]{2,1,0:T(8,128)} async-done(((f32[16,192,384]{2,1,0:T(8,128)}), f32[16,192,384]{2,1,0:T(8,128)}, u32[]{:S(2)}, u32[]{:S(2)}) %all-to-all-start) | async-done | bytes 4718624 | tf_op jit(solution)/shard_map/all_to_all | solution.py:59
  323.9 2.6 reduce_sum.9
  330.6 1.5 convolution_subtract_fusion.1
  333.3 1.9 dynamic-slice_reduce_fusion
  335.3 2.1 all_gather_reshape.7
  338.5 52.8 %all-gather.8.cloned.1.call-done = f32[16,512,192]{1,2,0:T(8,128)} async-done(((f32[1,512,192]{1,2,0:T(8,128)}), f32[16,512,192]{1,2,0:T(8,128)}) %all-gather.8.cloned.1.call-update) | async-done | bytes 6291472 | tf_op jit(solution)/shard_map/all_gather | solution.py:31
  391.3 1.0 dynamic-slice_bitcast_fusion
  392.4 6.0 %bitcast_subtract_fusion = f32[1024,512]{1,0:T(8,128)} fusion(f32[128,8,4,128]{3,2,1,0:T(4,128)S(1)} %bitcast.98, f32[1024,96]{0,1:T(8,128)} %copy-done.2, f32[1024,96]{0,1:T(8,128)S(1)} %fusion.19, f32[1024,96]{0,1:T(8,128)S(1)} %copy.62, f32[1024,96]{0,1:T(8,128)} %copy.61, f32[512,96]{0,1:T(8,128)} %copy-done.4, f32[512,96]{0,1:T(8,128)} %copy-done.3, ...), kind=kOutput, calls=%fused_computation | convolution fusion | flops 2418016256 | bytes 6553600 | tf_op jit(solution)/shard_map/dot_general | solution.py:95
  398.4 2.9 reshape.29
  (46 shorter events, 10.6 us)
Async XLA Ops:
  6.5 99.5 %all-gather.6.cloned.1.call-start = ((), (), s32[]{:S(2)}) async-start(), calls=%async_computation.3 | async-start | bytes 6684672 | tf_op jit(solution)/shard_map/all_gather | solution.py:31
  48.8 59.0 %copy-start = (f32[8,1,128,4,1,128]{5,4,3,2,1,0:T(1,128)S(1)}, f32[8,1,128,4,1,128]{5,4,3,2,1,0:T(1,128)}, u32[]{:S(2)}) copy-start(f32[8,1,128,4,1,128]{5,4,3,2,1,0:T(1,128)} %param.3) | copy-start | bytes 6291460
  51.7 122.6 %reduce-scatter.3.cloned.1.call-start = ((), (), s32[]{:S(2)}) async-start(), calls=%async_computation.4 | async-start | bytes 1114112 | tf_op jit(solution)/shard_map/reduce_scatter | solution.py:45
  107.0 0.7 copy-start.3
  107.1 0.7 copy-start.4
  113.5 93.0 %reduce-scatter.5.cloned.1.call-start = ((), (), s32[]{:S(2)}) async-start(), calls=%async_computation.5 | async-start | bytes 98304 | tf_op jit(solution)/shard_map/reduce_scatter | solution.py:45
  248.3 13.7 %copy-start.5 = (f32[2,96,96]{2,1,0:T(8,128)S(1)}, f32[2,96,96]{2,1,0:T(8,128)}, u32[]{:S(2)}) copy-start(f32[2,96,96]{2,1,0:T(8,128)} %param.5) | copy-start | bytes 221188
  248.3 75.6 %all-to-all-start = ((f32[16,192,384]{2,1,0:T(8,128)}), f32[16,192,384]{2,1,0:T(8,128)}, u32[]{:S(2)}, u32[]{:S(2)}) async-start(f32[16,192,384]{2,1,0:T(8,128)} %broadcast_in_dim.3), calls=%async_computation.2 | async-start | bytes 9437184 | tf_op jit(solution)/shard_map/all_to_all | solution.py:59
  261.4 129.9 %all-gather.8.cloned.1.call-start = ((), (), s32[]{:S(2)}) async-start(), calls=%async_computation.6 | async-start | bytes 6684672 | tf_op jit(solution)/shard_map/all_gather | solution.py:31
  326.5 3.2 copy-start.6
  332.6 0.8 copy-start.2
  335.3 57.1 %copy-start.1 = (f32[8,1,128,4,1,128]{5,4,3,2,1,0:T(1,128)S(1)}, f32[8,1,128,4,1,128]{5,4,3,2,1,0:T(1,128)}, u32[]{:S(2)}) copy-start(f32[8,1,128,4,1,128]{5,4,3,2,1,0:T(1,128)} %param.3) | copy-start | bytes 6291460
Sparse Core Ops, SparseCore 0:
  51.8 54.1 all-gather.5
  113.6 60.6 reduce-scatter.2
  177.3 29.2 reduce-scatter.4
  337.5 53.7 all-gather.7
where the time goes:
time: 408 us
  waiting for transfers between devices  261 us (64%)
  blocking collectives  77.4 us (19%)
  local copies, waits for them, and re-layouts  21.1 us (5%)
  matrix products  18.8 us (5%)
  starting transfers between devices  13.4 us (3%)
  between operations  13.4 us (3%)
    all_gather x2, waiting for transfers between devices, from_root(): lax.all_gather(array, axis)  107 us
    reduce_scatter x2, waiting for transfers between devices, reduced_to_own(): tiles = lax.psum_scatter(tiles, axes[k], scatter_dimension=0, tiled=True)  92.8 us
    all_gather x4, blocking collectives, stacked_from(): tiles = lax.all_gather(tiles, axes[k])  77.4 us
    all_to_all x1, waiting for transfers between devices, sent_to_all(): return lax.all_to_all(copies, axis, split_axis=0, concat_axis=0, tiled=True)  61.2 us
    all_to_all x1, starting transfers between devices, sent_to_all(): return lax.all_to_all(copies, axis, split_axis=0, concat_axis=0, tiled=True)  13.1 us
    dot_general x15, matrix products, product(): jnp.dot(matrix_a, matrix_b, precision=lax.Precision.HIGHEST, preferred_el...  9.86 us
  transfers between devices with their start and end apart: 5, of which 5 were waited for; matrix products, arithmetic and copies ran while one was open for 1% of the time, Pallas kernels for 0%

commit v1 on v0

v1 whole, which is shorter than its diff:
```python
import jax
import jax.numpy as jnp
from jax import lax
from jax.experimental import pallas as pl
from jax.experimental.pallas import tpu as pltpu
from jax.sharding import Mesh
from jax.sharding import PartitionSpec as P

ROWS = 16
ZS = 16
XS = 2
W = 96
LANES = 128
SLICE = 48
PART = 24
BLOCK = 72


def dot(a, b, ca=1, cb=0):
    return lax.dot_general(
        a,
        b,
        (((ca,), (cb,)), ((), ())),
        precision=lax.Precision.HIGHEST,
        preferred_element_type=jnp.float32,
    )


def call(kernel, outs, scratch, flops, *args):
    shapes = [jax.ShapeDtypeStruct(s, jnp.float32) for s in outs]
    moved = sum(x.size for x in list(args) + shapes) * 4
    return pl.pallas_call(
        kernel,
        out_shape=shapes,
        in_specs=[pl.BlockSpec(memory_space=pltpu.VMEM)] * len(args),
        out_specs=[pl.BlockSpec(memory_space=pltpu.VMEM)] * len(outs),
        scratch_shapes=[pltpu.VMEM(s, jnp.float32) for s in scratch],
        compiler_params=pltpu.CompilerParams(vmem_limit_bytes=40 * 1024 * 1024),
        cost_estimate=pl.CostEstimate(flops=flops, bytes_accessed=moved, transcendentals=0),
    )(*args)


def pack_kernel(v_ref, all_ref, own_ref, other_ref):
    xh = lax.axis_index("xh")
    first = [jnp.concatenate([v_ref[0, i], v_ref[1, i][:, :32]], axis=1) for i in range(8)]
    rest = [v_ref[1, i][:, 32:] for i in range(8)]
    pairs = [jnp.concatenate([rest[i], rest[i + 4]], axis=1) for i in range(4)]
    block = jnp.concatenate(first + pairs, axis=0)
    for k in range(ZS):
        all_ref[k] = block
    halves = []
    for h in range(2):
        low = [jnp.concatenate([rest[2 * j + h], rest[2 * j + 4 + h]], axis=1) for j in range(2)]
        halves.append(jnp.concatenate([first[2 * j + h] for j in range(4)] + low, axis=0))
    is_low = xh == 0
    own_ref[...] = jnp.where(is_low, halves[0], halves[1])
    other_ref[...] = jnp.where(is_low, halves[1], halves[0])


def image_kernel(a_ref, g_ref, own_ref, other_ref, send_ref, va_ref, vb_ref):
    xh = lax.axis_index("xh")
    for i in range(8):
        for r in range(4):
            va_ref[pl.ds(i * 128 + r, 32, stride=4), :] = g_ref[
                pl.ds(i * 4 + r, 32, stride=SLICE), :
            ]
    for i in range(4):
        for r in range(4):
            both = g_ref[pl.ds(32 + i * 4 + r, 32, stride=SLICE), :]
            vb_ref[pl.ds(i * 128 + r, 32, stride=4), :] = both
            vb_ref[pl.ds((i + 4) * 128 + r, 32, stride=4), :] = pltpu.roll(both, 64, 1)
    v = jnp.concatenate([va_ref[...], vb_ref[:, :64]], axis=1)
    for half in range(2):
        tiles = [a_ref[pl.ds(2 * half + t, 1024, stride=4), :] for t in range(2)]
        q = dot(v, jnp.concatenate(tiles, axis=1), 0, 0)
        for t in range(2):
            j = 2 * half + t
            for kk in range(12):
                send_ref[pl.ds(kk * 4 + j, 16, stride=2 * SLICE), :] = q[
                    kk * 16 : kk * 16 + 16, t * 128 : t * 128 + 128
                ]
    is_low = xh == 0
    zero = jnp.where(is_low, own_ref[...], other_ref[...])
    one = jnp.where(is_low, other_ref[...], own_ref[...])
    for k in range(ROWS):
        send_ref[k * 96 + 48 : k * 96 + 72, :] = zero
        send_ref[k * 96 + 72 : k * 96 + 96, :] = one


def slice_kernel(r_ref, block_ref, y_ref, va_ref, vb_ref, sum_ref):
    me = lax.axis_index("row")
    total = r_ref[0:48, :]
    for k in range(1, ROWS):
        total = total + r_ref[k * 96 : k * 96 + 48, :]
    sum_ref[...] = total
    for x in range(XS):
        for j in range(4):
            for r in range(4):
                va_ref[pl.ds(j * 128 + x * 64 + r, 16, stride=4), :] = r_ref[
                    pl.ds(48 + x * 24 + j * 4 + r, 16, stride=96), :
                ]
        for j in range(2):
            for r in range(4):
                both = r_ref[pl.ds(64 + x * 24 + j * 4 + r, 16, stride=96), :]
                vb_ref[pl.ds(j * 128 + x * 64 + r, 16, stride=4), :] = both
                vb_ref[pl.ds((j + 2) * 128 + x * 64 + r, 16, stride=4), :] = pltpu.roll(both, 64, 1)
    v = jnp.concatenate([va_ref[...], vb_ref[:, :64]], axis=1)
    y = jnp.concatenate([sum_ref[pl.ds(j, 12, stride=4), :] for j in range(4)], axis=1)
    ht = dot(y, v)
    gram = dot(v[:, :W], v[:, W:], 0, 0)
    at = lax.broadcasted_iota(jnp.int32, (8, W), 0) * 16 + me
    pick = jnp.where(at == lax.broadcasted_iota(jnp.int32, (8, W), 1), 1.0, 0.0)
    mine = dot(pick, gram)
    low = jnp.concatenate([ht[0:6, 128:], ht[6:12, 128:]], axis=1)
    mine = jnp.concatenate([mine[0:6], jnp.zeros((6, 32), jnp.float32)], axis=1)
    tail = jnp.concatenate([ht[:, :128], low, mine], axis=0)
    for k in range(ZS):
        block_ref[k, 0:48, :] = total
        block_ref[k, 48:72, :] = tail
        y_ref[k] = total


def turn_kernel(r_ref, out_ref):
    tail = r_ref[0, 48:72, :]
    for k in range(1, ZS):
        tail = tail + r_ref[k, 48:72, :]
    for k in range(ROWS):
        for x in range(XS):
            out_ref[2 * k + x, 0:48, :] = r_ref[k, 0:48, :]
            out_ref[2 * k + x, 48:72, :] = tail


def update_kernel(
    a_ref, vra_ref, vrb_ref, vca_ref, vcb_ref, y_ref, r_ref, t_ref, out_ref, yr_ref, yc_ref
):
    def both(start):
        here = r_ref[pl.ds(start, 16, stride=2 * BLOCK), :]
        return here + r_ref[pl.ds(start + BLOCK, 16, stride=2 * BLOCK), :]

    wide = [both(48 + k) for k in range(12)]
    low = [both(60 + k) for k in range(6)]
    h_a = jnp.concatenate(wide, axis=0)
    h_b = jnp.concatenate([x[:, :64] for x in low] + [x[:, 64:] for x in low], axis=0)
    ht = jnp.concatenate([h_a, h_b], axis=1)
    g = jnp.concatenate([both(66 + k) for k in range(6)], axis=0)[:, :W]
    for k in range(12):
        for j in range(4):
            for x in range(XS):
                i = 2 * j + x
                yr_ref[k * 16 : k * 16 + 16, i * 128 : i * 128 + 128] = r_ref[
                    pl.ds(x * BLOCK + k * 4 + j, 16, stride=2 * BLOCK), :
                ]
            yc_ref[k * 16 : k * 16 + 16, j * 128 : j * 128 + 128] = y_ref[
                pl.ds(k * 4 + j, 16, stride=SLICE), :
            ]
    t1 = t_ref[0]
    t2 = t_ref[1]
    shift1 = 0.5 * dot(t1, dot(ht[:W, :W], t1), 0, 0)
    crossed = dot(t1, ht[:W, W:], 0, 0) - dot(shift1, g, 0, 0)
    fold = dot(g, crossed, 0, 0)
    second = ht[W:, W:] - fold - fold.T
    shift2 = 0.5 * dot(t2, dot(second, t2), 0, 0)
    gt = dot(g, t2)
    corner = dot(crossed, t2) - dot(shift1, gt)
    none = jnp.zeros((W, W), jnp.float32)
    left = jnp.concatenate(
        [
            jnp.concatenate([t1, -dot(t1, gt)], axis=1),
            jnp.concatenate([none, t2], axis=1),
        ],
        axis=0,
    )
    sym = jnp.concatenate(
        [
            jnp.concatenate([shift1 + shift1.T, corner], axis=1),
            jnp.concatenate([corner.T, shift2 + shift2.T], axis=1),
        ],
        axis=0,
    )
    vc = jnp.concatenate([vca_ref[...], vcb_ref[:, :64]], axis=1)
    m1 = dot(left, yc_ref[...], 0, 0) - dot(sym, vc, 1, 1)
    m2 = dot(left, vc, 1, 1)
    for i in range(8):
        at = i * 128
        vr = jnp.concatenate([vra_ref[at : at + 128, :], vrb_ref[at : at + 128, :64]], axis=1)
        change = dot(vr, m1) + dot(yr_ref[:, at : at + 128], m2, 0, 0)
        for j in range(4):
            where = pl.ds(at * 4 + j, 128, stride=4)
            out_ref[where, :] = a_ref[where, :] - change[:, j * 128 : j * 128 + 128]


def spread(array, axes):
    return lax.all_to_all(array, axes, split_axis=0, concat_axis=0, tiled=True)


def shards(matrix, vectors, factors):
    blocks = matrix.reshape(-1, LANES)
    every = [(p, x, z) for p in range(ROWS) for x in range(XS) for z in range(ZS)]
    number = {at: k for k, at in enumerate(every)}
    same = [(number[p, x, z], number[z, x, p]) for p, x, z in every]
    cross = [(number[p, x, z], number[z, 1 - x, p]) for p, x, z in every]
    whole = ("row", "xh", "z")

    sent, own, other = call(
        pack_kernel,
        [(ZS, SLICE, LANES), (PART, LANES), (PART, LANES)],
        [],
        0,
        vectors.reshape(2, 8, 4, W),
    )
    own = lax.ppermute(own, whole, same)
    other = lax.ppermute(other, whole, cross)
    column = spread(sent, "z").reshape(ZS * SLICE, LANES)
    gathered = lax.all_gather(column, "xh", axis=0, tiled=True)
    image, vra, vrb = call(
        image_kernel,
        [(ROWS * 96, LANES), (1024, LANES), (1024, LANES)],
        [],
        2 * 1024 * 512 * 192,
        blocks,
        gathered,
        own,
        other,
    )
    image = spread(image.reshape(ROWS, 96, LANES), "row").reshape(-1, LANES)
    block, mine, vca, vcb = call(
        slice_kernel,
        [(ZS, BLOCK, LANES), (ROWS, SLICE, LANES), (512, LANES), (512, LANES)],
        [(SLICE, LANES)],
        2 * 512 * 192 * 96,
        image,
    )
    y_cols = spread(mine, "row").reshape(-1, LANES)
    block = spread(block, "z")
    (block,) = call(turn_kernel, [(2 * ROWS, BLOCK, LANES)], [], 0, block)
    y_rows = spread(block, ("row", "xh")).reshape(-1, LANES)
    (out,) = call(
        update_kernel,
        [(4096, LANES)],
        [(192, 1024), (192, 512)],
        2 * 1024 * 512 * 384,
        blocks,
        vra,
        vrb,
        vca,
        vcb,
        y_cols,
        y_rows,
        factors,
    )
    return out.reshape(matrix.shape)


def solution(mesh):
    finer = Mesh(mesh.devices.reshape(ROWS, XS, ZS), ("row", "xh", "z"))
    cols = ("xh", "z")
    placed = (P(None, "row", None, None, cols, None), P(None, None, "row", cols, None), P())
    return jax.shard_map(
        shards,
        mesh=finer,
        in_specs=placed,
        out_specs=placed[0],
        check_vma=False,
    )
```

time: 408 us -> 167 us (0.41)
  waiting for transfers between devices: 261 us -> 16.8 us
  blocking collectives: 77.4 us -> 100 us
  starting transfers between devices: 13.4 us -> 32.6 us
  matrix products: 18.8 us -> 0 us
  local copies, waits for them, and re-layouts: 21.1 us -> 3.44 us
  Pallas kernels: 0 us -> 13.4 us
  between operations: 13.4 us -> 0.1 us
    all_gather x2 -> x0, waiting for transfers between devices: 107 us -> none  [from_root(): lax.all_gather(array, axis)]
    reduce_scatter x2 -> x0, waiting for transfers between devices: 92.8 us -> none  [reduced_to_own(): tiles = lax.psum_scatter(tiles, axes[k], scatter_dimension=0, tiled=True)]
    all_to_all x0 -> x3, blocking collectives: none -> 90 us  [spread(): return lax.all_to_all(array, axes, split_axis=0, concat_axis=0, tiled=True)]
    all_gather x4 -> x1, blocking collectives: 77.4 us -> 10.3 us  [shards(): gathered = lax.all_gather(column, 'xh', axis=0, tiled=True)]
    all_to_all x1 -> x2, waiting for transfers between devices: 61.2 us -> 16.8 us  [spread(): return lax.all_to_all(array, axes, split_axis=0, concat_axis=0, tiled=True)]
    dot_general x17 -> x0, matrix products: 18.8 us -> none  [the longest x15 9.86 us: product(): jnp.dot(matrix_a, matrix_b, precision=lax.Precision.HIGHEST, preferred_el...]
    pallas_call x0 -> x5, Pallas kernels: none -> 13.4 us  [call(): pl.pallas_call(kernel, out_shape=shapes, in_specs=[pl.BlockSpec(memory_sp...]
    all_to_all x1 -> x2, starting transfers between devices: 13.1 us -> 23.8 us  [spread(): return lax.all_to_all(array, axes, split_axis=0, concat_axis=0, tiled=True)]
  transfers between devices with their start and end apart: 5 -> 4, of which waited for: 5 -> 2; matrix products, arithmetic and copies ran while one was open for 1% -> 0% of each run, Pallas kernels for 0% -> 0%
where the time goes in v1:
time: 167 us
  blocking collectives  100 us (60%)
  starting transfers between devices  32.6 us (20%)
  waiting for transfers between devices  16.8 us (10%)
  Pallas kernels  13.4 us (8%)
  local copies, waits for them, and re-layouts  3.44 us (2%)
    all_to_all x3, blocking collectives, spread(): return lax.all_to_all(array, axes, split_axis=0, concat_axis=0, tiled=True)  90 us
    all_to_all x2, starting transfers between devices, spread(): return lax.all_to_all(array, axes, split_axis=0, concat_axis=0, tiled=True)  23.8 us
    all_to_all x2, waiting for transfers between devices, spread(): return lax.all_to_all(array, axes, split_axis=0, concat_axis=0, tiled=True)  16.8 us
    pallas_call x5, Pallas kernels, call(): pl.pallas_call(kernel, out_shape=shapes, in_specs=[pl.BlockSpec(memory_sp...  13.4 us
    all_gather x1, blocking collectives, shards(): gathered = lax.all_gather(column, 'xh', axis=0, tiled=True)  10.3 us
    ppermute x1, starting transfers between devices, shards(): own = lax.ppermute(own, whole, same)  4.38 us
    ppermute x1, starting transfers between devices, shards(): other = lax.ppermute(other, whole, cross)  4.38 us
    unnamed x22, local copies, waits for them, and re-layouts  3.44 us
  transfers between devices with their start and end apart: 4, of which 2 were waited for; matrix products, arithmetic and copies ran while one was open for 0% of the time, Pallas kernels for 0%

profile of v1, /device:TPU:1, one launch (start us, length us, event | category | flops | bytes accessed | tf_op | source)
XLA Modules:
  0.0 166.6 jit_solution(9572731220906368358)
XLA Ops:
  0.0 0.8 copy-done.10
  0.8 0.8 shard_map.37
  1.6 15.7 %all-to-all-start = ((f32[16,48,128]{2,1,0:T(8,128)}), f32[16,48,128]{2,1,0:T(8,128)S(1)}, u32[]{:S(2)}, u32[]{:S(2)}) async-start(f32[16,48,128]{2,1,0:T(8,128)} %get-tuple-element.15), calls=%async_computation | async-start | bytes 786432 | tf_op jit(solution)/shard_map/all_to_all | solution.py:193
  17.4 4.4 %collective-permute-start = (f32[24,128]{1,0:T(8,128)S(1)}, f32[24,128]{1,0:T(8,128)S(1)}, u32[]{:S(2)}, u32[]{:S(2)}) collective-permute-start(f32[24,128]{1,0:T(8,128)S(1)} %get-tuple-element.16), channel_id=1, source_target_pairs={{0,0},{1,32},{2,64},{3,96},{4,128},{5,160},{6,192},{7,224},{8,256}... | collective-permute-start | bytes 36872 | tf_op jit(solution)/shard_map/ppermute | solution.py:211
  21.7 4.4 %collective-permute-start.1 = (f32[24,128]{1,0:T(8,128)S(1)}, f32[24,128]{1,0:T(8,128)S(1)}, u32[]{:S(2)}, u32[]{:S(2)}) collective-permute-start(f32[24,128]{1,0:T(8,128)S(1)} %get-tuple-element.17), channel_id=1, source_target_pairs={{0,16},{1,48},{2,80},{3,112},{4,144},{5,176},{6,208},{7,240},{8,27... | collective-permute-start | bytes 36872 | tf_op jit(solution)/shard_map/ppermute | solution.py:212
  26.1 9.4 %all-to-all-done = f32[16,48,128]{2,1,0:T(8,128)S(1)} async-done(((f32[16,48,128]{2,1,0:T(8,128)}), f32[16,48,128]{2,1,0:T(8,128)S(1)}, u32[]{:S(2)}, u32[]{:S(2)}) %all-to-all-start) | async-done | bytes 393248 | tf_op jit(solution)/shard_map/all_to_all | solution.py:193
  35.5 10.3 %all_gather.3.g_ref = f32[1536,128]{1,0:T(8,128)S(1)} all-gather(f32[768,128]{1,0:T(8,128)S(1)} %bitcast.16), channel_id=1, replica_groups=mesh['row'=16,'xh'=2,'z'=16] {'xh'}, dimensions={0}, use_global_device_ids=true | all-gather | bytes 1179648 | tf_op jit(solution)/shard_map/all_gather | solution.py:214
  45.9 0.0 collective-permute-done.own_ref
  45.9 0.0 collective-permute-done.1.other_ref
  45.9 1.6 copy-done
  47.5 2.0 %shard_map.38 = (f32[1536,128]{1,0:T(8,128)S(1)}, f32[1024,128]{1,0:T(8,128)S(1)}, f32[1024,128]{1,0:T(8,128)S(1)}) custom-call(f32[4096,128]{1,0:T(8,128)S(1)} %bitcast.10, f32[1536,128]{1,0:T(8,128)S(1)} %all_gather.3.g_ref, f32[24,128]{1,0:T(8,128)S(1)} %collective-permute-done.own_ref, f32[24,128]{1,0:T(8,128)S(1)} %collective-permute-done.1.other_ref), custom_call_target="tpu_custom_call" | custom-call | flops 201326592 | bytes 4743168 | tf_op jit(solution)/shard_map/pallas_call | solution.py:32
  49.5 0.0 copy-start.3
  49.5 0.0 copy-start.5
  49.5 24.9 %all_to_all.25 = f32[16,96,128]{2,1,0:T(8,128)S(1)} all-to-all(f32[16,96,128]{2,1,0:T(8,128)S(1)} %bitcast.14), channel_id=1, replica_groups=mesh['row'=16,'xh'=2,'z'=16] {'row'}, dimensions={0} | all-to-all | bytes 1572864 | tf_op jit(solution)/shard_map/all_to_all | solution.py:193
  74.4 1.3 shard_map.39
  75.7 40.2 %all_to_all.26.r_ref = f32[16,72,128]{2,1,0:T(8,128)} all-to-all(f32[16,72,128]{2,1,0:T(8,128)S(1)} %get-tuple-element.24), channel_id=1, replica_groups=mesh['row'=16,'xh'=2,'z'=16] {'z'}, dimensions={0} | all-to-all | bytes 1179648 | tf_op jit(solution)/shard_map/all_to_all | solution.py:193
  115.9 0.0 copy-done.5
  115.9 8.1 %all-to-all-start.2 = ((f32[16,48,128]{2,1,0:T(8,128)}), f32[16,48,128]{2,1,0:T(8,128)}, u32[]{:S(2)}, u32[]{:S(2)}) async-start(f32[16,48,128]{2,1,0:T(8,128)} %get-tuple-element.23), calls=%async_computation.2 | async-start | bytes 786432 | tf_op jit(solution)/shard_map/all_to_all | solution.py:193
  124.0 1.1 copy-done.2
  125.0 0.1 shard_map.40
  125.1 7.4 %all-to-all-done.2 = f32[16,48,128]{2,1,0:T(8,128)} async-done(((f32[16,48,128]{2,1,0:T(8,128)}), f32[16,48,128]{2,1,0:T(8,128)}, u32[]{:S(2)}, u32[]{:S(2)}) %all-to-all-start.2) | async-done | bytes 393248 | tf_op jit(solution)/shard_map/all_to_all | solution.py:193
  132.6 24.9 %all_to_all.27 = f32[32,72,128]{2,1,0:T(8,128)S(1)} all-to-all(f32[32,72,128]{2,1,0:T(8,128)S(1)} %shard_map.40), channel_id=1, replica_groups=mesh['row'=16,'xh'=2,'z'=16] {'row','xh'}, dimensions={0} | all-to-all | bytes 2359296 | tf_op jit(solution)/shard_map/all_to_all | solution.py:193
  157.5 0.0 copy-done.4
  157.5 9.1 %shard_map.41 = f32[4096,128]{1,0:T(8,128)} custom-call(f32[4096,128]{1,0:T(8,128)S(1)} %bitcast.11, f32[1024,128]{1,0:T(8,128)S(1)} %copy-done.4, f32[1024,128]{1,0:T(8,128)S(1)} %copy-done.6, f32[512,128]{1,0:T(8,128)S(1)} %get-tuple-element.21.vca_ref, f32[512,128]{1,0:T(8,128)S(1)} %copy-done.8, f32[768,128]{1,0:T(8,128)} %bitcast.5.y_ref, ...), custom_call_target="tpu_custom_call" | custom-call | flops 402653184 | bytes 7413760 | tf_op jit(solution)/shard_map/pallas_call | solution.py:32
  (15 shorter events, 0.0 us)
Async XLA Ops:
  0.0 0.8 copy-start.10
  1.6 33.9 %all-to-all-start = ((f32[16,48,128]{2,1,0:T(8,128)}), f32[16,48,128]{2,1,0:T(8,128)S(1)}, u32[]{:S(2)}, u32[]{:S(2)}) async-start(f32[16,48,128]{2,1,0:T(8,128)} %get-tuple-element.15), calls=%async_computation | async-start | bytes 786432 | tf_op jit(solution)/shard_map/all_to_all | solution.py:193
  17.4 28.5 %collective-permute-start = (f32[24,128]{1,0:T(8,128)S(1)}, f32[24,128]{1,0:T(8,128)S(1)}, u32[]{:S(2)}, u32[]{:S(2)}) collective-permute-start(f32[24,128]{1,0:T(8,128)S(1)} %get-tuple-element.16), channel_id=1, source_target_pairs={{0,0},{1,32},{2,64},{3,96},{4,128},{5,160},{6,192},{7,224},{8,256}... | collective-permute-start | bytes 36872 | tf_op jit(solution)/shard_map/ppermute | solution.py:211
  21.7 24.1 %collective-permute-start.1 = (f32[24,128]{1,0:T(8,128)S(1)}, f32[24,128]{1,0:T(8,128)S(1)}, u32[]{:S(2)}, u32[]{:S(2)}) collective-permute-start(f32[24,128]{1,0:T(8,128)S(1)} %get-tuple-element.17), channel_id=1, source_target_pairs={{0,16},{1,48},{2,80},{3,112},{4,144},{5,176},{6,208},{7,240},{8,27... | collective-permute-start | bytes 36872 | tf_op jit(solution)/shard_map/ppermute | solution.py:212
  45.9 1.6 copy-start
  49.5 66.4 %copy-start.3 = (f32[1024,128]{1,0:T(8,128)}, f32[1024,128]{1,0:T(8,128)S(1)}, u32[]{:S(2)}) copy-start(f32[1024,128]{1,0:T(8,128)S(1)} %get-tuple-element.18.vra_ref) | copy-start | bytes 1572868
  49.5 66.4 %copy-start.5 = (f32[1024,128]{1,0:T(8,128)}, f32[1024,128]{1,0:T(8,128)S(1)}, u32[]{:S(2)}) copy-start(f32[1024,128]{1,0:T(8,128)S(1)} %get-tuple-element.19.vrb_ref) | copy-start | bytes 1572868
  75.7 40.2 %copy-start.7 = (f32[512,128]{1,0:T(8,128)}, f32[512,128]{1,0:T(8,128)S(1)}, u32[]{:S(2)}) copy-start(f32[512,128]{1,0:T(8,128)S(1)} %get-tuple-element.22.vcb_ref) | copy-start | bytes 786436
  115.9 16.7 %all-to-all-start.2 = ((f32[16,48,128]{2,1,0:T(8,128)}), f32[16,48,128]{2,1,0:T(8,128)}, u32[]{:S(2)}, u32[]{:S(2)}) async-start(f32[16,48,128]{2,1,0:T(8,128)} %get-tuple-element.23), calls=%async_computation.2 | async-start | bytes 786432 | tf_op jit(solution)/shard_map/all_to_all | solution.py:193
  124.0 1.1 copy-start.2
  125.0 32.4 %copy-start.1 = (f32[8,1,128,4,1,128]{5,4,3,2,1,0:T(1,128)S(1)}, f32[8,1,128,4,1,128]{5,4,3,2,1,0:T(1,128)}, u32[]{:S(2)}) copy-start(f32[8,1,128,4,1,128]{5,4,3,2,1,0:T(1,128)} %param.3) | copy-start | bytes 6291460
  132.6 24.9 %copy-start.4 = (f32[1024,128]{1,0:T(8,128)S(1)}, f32[1024,128]{1,0:T(8,128)}, u32[]{:S(2)}) copy-start(f32[1024,128]{1,0:T(8,128)} %copy-done.3) | copy-start | bytes 1572868
  132.6 24.9 %copy-start.6 = (f32[1024,128]{1,0:T(8,128)S(1)}, f32[1024,128]{1,0:T(8,128)}, u32[]{:S(2)}) copy-start(f32[1024,128]{1,0:T(8,128)} %copy-done.5) | copy-start | bytes 1572868
  132.6 24.9 %copy-start.8 = (f32[512,128]{1,0:T(8,128)S(1)}, f32[512,128]{1,0:T(8,128)}, u32[]{:S(2)}) copy-start(f32[512,128]{1,0:T(8,128)} %copy-done.7) | copy-start | bytes 786436
  132.6 24.9 %copy-start.9 = (f32[2,96,96]{2,1,0:T(8,128)S(1)}, f32[2,96,96]{2,1,0:T(8,128)}, u32[]{:S(2)}) copy-start(f32[2,96,96]{2,1,0:T(8,128)} %t_ref.1) | copy-start | bytes 221188

commit v2 on v1

--- a/solution.py
+++ b/solution.py
@@ -40,35 +40,36 @@
     )(*args)
 
 
-def pack_kernel(v_ref, all_ref, own_ref, other_ref):
-    xh = lax.axis_index("xh")
+def pack_kernel(v_ref, out_ref):
     first = [jnp.concatenate([v_ref[0, i], v_ref[1, i][:, :32]], axis=1) for i in range(8)]
     rest = [v_ref[1, i][:, 32:] for i in range(8)]
-    pairs = [jnp.concatenate([rest[i], rest[i + 4]], axis=1) for i in range(4)]
-    block = jnp.concatenate(first + pairs, axis=0)
-    for k in range(ZS):
-        all_ref[k] = block
-    halves = []
+    parts = []
     for h in range(2):
-        low = [jnp.concatenate([rest[2 * j + h], rest[2 * j + 4 + h]], axis=1) for j in range(2)]
-        halves.append(jnp.concatenate([first[2 * j + h] for j in range(4)] + low, axis=0))
-    is_low = xh == 0
-    own_ref[...] = jnp.where(is_low, halves[0], halves[1])
-    other_ref[...] = jnp.where(is_low, halves[1], halves[0])
-
-
-def image_kernel(a_ref, g_ref, own_ref, other_ref, send_ref, va_ref, vb_ref):
-    xh = lax.axis_index("xh")
-    for i in range(8):
-        for r in range(4):
-            va_ref[pl.ds(i * 128 + r, 32, stride=4), :] = g_ref[
-                pl.ds(i * 4 + r, 32, stride=SLICE), :
-            ]
-    for i in range(4):
-        for r in range(4):
-            both = g_ref[pl.ds(32 + i * 4 + r, 32, stride=SLICE), :]
-            vb_ref[pl.ds(i * 128 + r, 32, stride=4), :] = both
-            vb_ref[pl.ds((i + 4) * 128 + r, 32, stride=4), :] = pltpu.roll(both, 64, 1)
+        parts += [first[2 * j + h] for j in range(4)]
+        parts += [
+            jnp.concatenate([rest[2 * j + h], rest[2 * j + 4 + h]], axis=1) for j in range(2)
+        ]
+    out_ref[...] = jnp.concatenate(parts, axis=0)
+
+
+def image_kernel(a_ref, g_ref, own_ref, send_ref, va_ref, vb_ref):
+    for x in range(XS):
+        for j in range(4):
+            for h in range(2):
+                for r in range(4):
+                    to = pl.ds((2 * j + h) * 128 + x * 64 + r, 16, stride=4)
+                    va_ref[to, :] = g_ref[
+                        pl.ds(x * SLICE + h * PART + j * 4 + r, 16, stride=2 * SLICE), :
+                    ]
+        for j in range(2):
+            for h in range(2):
+                for r in range(4):
+                    both = g_ref[
+                        pl.ds(x * SLICE + h * PART + 16 + j * 4 + r, 16, stride=2 * SLICE), :
+                    ]
+                    at = (2 * j + h) * 128 + x * 64 + r
+                    vb_ref[pl.ds(at, 16, stride=4), :] = both
+                    vb_ref[pl.ds(at + 512, 16, stride=4), :] = pltpu.roll(both, 64, 1)
     v = jnp.concatenate([va_ref[...], vb_ref[:, :64]], axis=1)
     for half in range(2):
         tiles = [a_ref[pl.ds(2 * half + t, 1024, stride=4), :] for t in range(2)]
@@ -79,12 +80,9 @@
                 send_ref[pl.ds(kk * 4 + j, 16, stride=2 * SLICE), :] = q[
                     kk * 16 : kk * 16 + 16, t * 128 : t * 128 + 128
                 ]
-    is_low = xh == 0
-    zero = jnp.where(is_low, own_ref[...], other_ref[...])
-    one = jnp.where(is_low, other_ref[...], own_ref[...])
+    own = own_ref[...]
     for k in range(ROWS):
-        send_ref[k * 96 + 48 : k * 96 + 72, :] = zero
-        send_ref[k * 96 + 72 : k * 96 + 96, :] = one
+        send_ref[k * 96 + 48 : k * 96 + 96, :] = own
 
 
 def slice_kernel(r_ref, block_ref, y_ref, va_ref, vb_ref, sum_ref):
@@ -114,9 +112,9 @@
     low = jnp.concatenate([ht[0:6, 128:], ht[6:12, 128:]], axis=1)
     mine = jnp.concatenate([mine[0:6], jnp.zeros((6, 32), jnp.float32)], axis=1)
     tail = jnp.concatenate([ht[:, :128], low, mine], axis=0)
-    for k in range(ZS):
-        block_ref[k, 0:48, :] = total
-        block_ref[k, 48:72, :] = tail
+    block_ref[0:48, :] = total
+    block_ref[48:72, :] = tail
+    for k in range(ROWS):
         y_ref[k] = total
 
 
@@ -198,20 +196,13 @@
     every = [(p, x, z) for p in range(ROWS) for x in range(XS) for z in range(ZS)]
     number = {at: k for k, at in enumerate(every)}
     same = [(number[p, x, z], number[z, x, p]) for p, x, z in every]
-    cross = [(number[p, x, z], number[z, 1 - x, p]) for p, x, z in every]
     whole = ("row", "xh", "z")
 
-    sent, own, other = call(
-        pack_kernel,
-        [(ZS, SLICE, LANES), (PART, LANES), (PART, LANES)],
-        [],
-        0,
-        vectors.reshape(2, 8, 4, W),
-    )
-    own = lax.ppermute(own, whole, same)
-    other = lax.ppermute(other, whole, cross)
-    column = spread(sent, "z").reshape(ZS * SLICE, LANES)
-    gathered = lax.all_gather(column, "xh", axis=0, tiled=True)
+    (packed,) = call(pack_kernel, [(SLICE, LANES)], [], 0, vectors.reshape(2, 8, 4, W))
+    pair = lax.all_gather(packed, "xh")
+    own = lax.dynamic_slice_in_dim(pair, lax.axis_index("xh") * PART, PART, axis=1)
+    own = lax.ppermute(own.reshape(SLICE, LANES), whole, same)
+    gathered = lax.all_gather(pair.reshape(2 * SLICE, LANES), "z", axis=0, tiled=True)
     image, vra, vrb = call(
         image_kernel,
         [(ROWS * 96, LANES), (1024, LANES), (1024, LANES)],
@@ -220,18 +211,17 @@
         blocks,
         gathered,
         own,
-        other,
     )
     image = spread(image.reshape(ROWS, 96, LANES), "row").reshape(-1, LANES)
     block, mine, vca, vcb = call(
         slice_kernel,
-        [(ZS, BLOCK, LANES), (ROWS, SLICE, LANES), (512, LANES), (512, LANES)],
+        [(BLOCK, LANES), (ROWS, SLICE, LANES), (512, LANES), (512, LANES)],
         [(SLICE, LANES)],
         2 * 512 * 192 * 96,
         image,
     )
     y_cols = spread(mine, "row").reshape(-1, LANES)
-    block = spread(block, "z")
+    block = lax.all_gather(block, "z")
     (block,) = call(turn_kernel, [(2 * ROWS, BLOCK, LANES)], [], 0, block)
     y_rows = spread(block, ("row", "xh")).reshape(-1, LANES)
     (out,) = call(

time: 167 us -> 148 us (0.89)
  starting transfers between devices: 32.6 us -> 10.4 us
  blocking collectives: 100 us -> 122 us
  waiting for transfers between devices: 16.8 us -> 0.01 us
    all_gather x1 -> x3, blocking collectives: 10.3 us -> 59.1 us  [the longest x1 30 us: shards(): lax.all_gather(pair.reshape(2 * SLICE, LANES), 'z', axis=0, tiled=True)]
    all_to_all x3 -> x2, blocking collectives: 90 us -> 62.5 us  [spread(): return lax.all_to_all(array, axes, split_axis=0, concat_axis=0, tiled=True)]
    all_to_all x2 -> x1, starting transfers between devices: 23.8 us -> 4.92 us  [spread(): return lax.all_to_all(array, axes, split_axis=0, concat_axis=0, tiled=True)]
    all_to_all x2 -> x1, waiting for transfers between devices: 16.8 us -> 0.01 us  [spread(): return lax.all_to_all(array, axes, split_axis=0, concat_axis=0, tiled=True)]
    ppermute x2 -> x1, starting transfers between devices: 8.76 us -> 5.49 us  [shards(): own = lax.ppermute(own.reshape(SLICE, LANES), whole, same)]
    unnamed x22 -> x20, local copies, waits for them, and re-layouts: 3.44 us -> 3.1 us
  transfers between devices with their start and end apart: 4 -> 2, of which waited for: 2 -> 0; matrix products, arithmetic and copies ran while one was open for 0% -> 0% of each run, Pallas kernels for 0% -> 0%
where the time goes in v2:
time: 148 us
  blocking collectives  122 us (82%)
  Pallas kernels  12.8 us (9%)
  starting transfers between devices  10.4 us (7%)
  local copies, waits for them, and re-layouts  3.1 us (2%)
    all_to_all x2, blocking collectives, spread(): return lax.all_to_all(array, axes, split_axis=0, concat_axis=0, tiled=True)  62.5 us
    all_gather x1, blocking collectives, shards(): lax.all_gather(pair.reshape(2 * SLICE, LANES), 'z', axis=0, tiled=True)  30 us
    all_gather x1, blocking collectives, shards(): block = lax.all_gather(block, 'z')  23.7 us
    pallas_call x5, Pallas kernels, call(): pl.pallas_call(kernel, out_shape=shapes, in_specs=[pl.BlockSpec(memory_sp...  12.8 us
    ppermute x1, starting transfers between devices, shards(): own = lax.ppermute(own.reshape(SLICE, LANES), whole, same)  5.49 us
    all_gather x1, blocking collectives, shards(): pair = lax.all_gather(packed, 'xh')  5.44 us
    all_to_all x1, starting transfers between devices, spread(): return lax.all_to_all(array, axes, split_axis=0, concat_axis=0, tiled=True)  4.92 us
    unnamed x20, local copies, waits for them, and re-layouts  3.1 us
  transfers between devices with their start and end apart: 2, of which 0 were waited for; matrix products, arithmetic and copies ran while one was open for 0% of the time, Pallas kernels for 0%

profile of v2, /device:TPU:1, one launch (start us, length us, event | category | flops | bytes accessed | tf_op | source)
XLA Modules:
  0.0 148.0 jit_solution(14175071954645172034)
XLA Ops:
  0.0 0.8 copy-done.9
  0.8 0.1 shard_map.37
  0.8 5.4 %all-gather = f32[96,128]{1,0:T(8,128)S(1)} all-gather(f32[48,128]{1,0:T(8,128)S(1)} %shard_map.37), channel_id=2, replica_groups=mesh['row'=16,'xh'=2,'z'=16] {'xh'}, dimensions={0}, use_global_device_ids=true | all-gather | bytes 73728 | tf_op jit(solution)/shard_map/all_gather | solution.py:202
  6.3 5.5 %collective-permute-start = (f32[48,128]{1,0:T(8,128)S(1)}, f32[48,128]{1,0:T(8,128)S(1)}, u32[]{:S(2)}, u32[]{:S(2)}) collective-permute-start(f32[48,128]{1,0:T(8,128)S(1)} %bitcast.20), channel_id=1, source_target_pairs={{0,0},{1,32},{2,64},{3,96},{4,128},{5,160},{6,192},{7,224},{8,256}... | collective-permute-start | bytes 73736 | tf_op jit(solution)/shard_map/ppermute | solution.py:204
  11.8 30.0 %all_gather.17.g_ref = f32[1536,128]{1,0:T(8,128)S(1)} all-gather(f32[96,128]{1,0:T(8,128)S(1)} %all-gather), channel_id=1, replica_groups=mesh['row'=16,'xh'=2,'z'=16] {'z'}, dimensions={0}, use_global_device_ids=true | all-gather | bytes 835584 | tf_op jit(solution)/shard_map/all_gather | solution.py:205
  41.7 0.0 collective-permute-done.own_ref
  41.7 1.6 %copy-done = f32[8,1,128,4,1,128]{5,4,3,2,1,0:T(1,128)S(1)} copy-done((f32[8,1,128,4,1,128]{5,4,3,2,1,0:T(1,128)S(1)}, f32[8,1,128,4,1,128]{5,4,3,2,1,0:T(1,128)}, u32[]{:S(2)}) %copy-start) | copy-done | bytes 2097176
  43.3 2.2 %shard_map.38 = (f32[1536,128]{1,0:T(8,128)S(1)}, f32[1024,128]{1,0:T(8,128)S(1)}, f32[1024,128]{1,0:T(8,128)S(1)}) custom-call(f32[4096,128]{1,0:T(8,128)S(1)} %bitcast.12, f32[1536,128]{1,0:T(8,128)S(1)} %all_gather.17.g_ref, f32[48,128]{1,0:T(8,128)S(1)} %collective-permute-done.own_ref), custom_call_target="tpu_custom_call" | custom-call | flops 201326592 | bytes 4743168 | tf_op jit(solution)/shard_map/pallas_call | solution.py:32
  45.5 0.0 copy-start.2
  45.6 0.0 copy-start.4
  45.6 29.5 %all_to_all.15 = f32[16,96,128]{2,1,0:T(8,128)S(1)} all-to-all(f32[16,96,128]{2,1,0:T(8,128)S(1)} %bitcast.17), channel_id=1, replica_groups=mesh['row'=16,'xh'=2,'z'=16] {'row'}, dimensions={0} | all-to-all | bytes 1572864 | tf_op jit(solution)/shard_map/all_to_all | solution.py:191
  75.0 1.3 shard_map.39
  76.3 0.0 copy-done.4
  76.3 0.7 copy-done.6
  77.0 4.9 %all-to-all-start.1 = ((f32[16,48,128]{2,1,0:T(8,128)}), f32[16,48,128]{2,1,0:T(8,128)}, u32[]{:S(2)}, u32[]{:S(2)}) async-start(f32[16,48,128]{2,1,0:T(8,128)} %get-tuple-element.17), calls=%async_computation.1 | async-start | bytes 786432 | tf_op jit(solution)/shard_map/all_to_all | solution.py:191
  82.0 23.7 %all-gather.1 = f32[1152,128]{1,0:T(8,128)S(1)} all-gather(f32[72,128]{1,0:T(8,128)S(1)} %get-tuple-element.18), channel_id=3, replica_groups=mesh['row'=16,'xh'=2,'z'=16] {'z'}, dimensions={0}, use_global_device_ids=true | all-gather | bytes 626688 | tf_op jit(solution)/shard_map/all_gather | solution.py:224
  105.7 0.1 shard_map.40
  105.8 0.0 all-to-all-done.1
  105.8 0.0 copy-start.3
  105.8 0.0 copy-start.8
  105.8 33.1 %all_to_all.16 = f32[32,72,128]{2,1,0:T(8,128)S(1)} all-to-all(f32[32,72,128]{2,1,0:T(8,128)S(1)} %shard_map.40), channel_id=1, replica_groups=mesh['row'=16,'xh'=2,'z'=16] {'row','xh'}, dimensions={0} | all-to-all | bytes 2359296 | tf_op jit(solution)/shard_map/all_to_all | solution.py:191
  138.9 0.0 copy-done.7
  138.9 0.0 copy-done.8
  138.9 9.1 %shard_map.41 = f32[4096,128]{1,0:T(8,128)} custom-call(f32[4096,128]{1,0:T(8,128)S(1)} %bitcast.13, f32[1024,128]{1,0:T(8,128)S(1)} %copy-done.3, f32[1024,128]{1,0:T(8,128)S(1)} %copy-done.5, f32[512,128]{1,0:T(8,128)S(1)} %get-tuple-element.15.vca_ref, f32[512,128]{1,0:T(8,128)S(1)} %copy-done.7, f32[768,128]{1,0:T(8,128)} %bitcast.6.y_ref, ...), custom_call_target="tpu_custom_call" | custom-call | flops 402653184 | bytes 7413760 | tf_op jit(solution)/shard_map/pallas_call | solution.py:32
  (11 shorter events, 0.0 us)
Async XLA Ops:
  0.0 0.8 copy-start.9
  6.3 35.5 %collective-permute-start = (f32[48,128]{1,0:T(8,128)S(1)}, f32[48,128]{1,0:T(8,128)S(1)}, u32[]{:S(2)}, u32[]{:S(2)}) collective-permute-start(f32[48,128]{1,0:T(8,128)S(1)} %bitcast.20), channel_id=1, source_target_pairs={{0,0},{1,32},{2,64},{3,96},{4,128},{5,160},{6,192},{7,224},{8,256}... | collective-permute-start | bytes 73736 | tf_op jit(solution)/shard_map/ppermute | solution.py:204
  41.7 1.6 %copy-start = (f32[8,1,128,4,1,128]{5,4,3,2,1,0:T(1,128)S(1)}, f32[8,1,128,4,1,128]{5,4,3,2,1,0:T(1,128)}, u32[]{:S(2)}) copy-start(f32[8,1,128,4,1,128]{5,4,3,2,1,0:T(1,128)} %param.3) | copy-start | bytes 6291460
  45.5 30.8 %copy-start.2 = (f32[1024,128]{1,0:T(8,128)}, f32[1024,128]{1,0:T(8,128)S(1)}, u32[]{:S(2)}) copy-start(f32[1024,128]{1,0:T(8,128)S(1)} %get-tuple-element.12.vra_ref) | copy-start | bytes 1572868
  45.6 30.8 %copy-start.4 = (f32[1024,128]{1,0:T(8,128)}, f32[1024,128]{1,0:T(8,128)S(1)}, u32[]{:S(2)}) copy-start(f32[1024,128]{1,0:T(8,128)S(1)} %get-tuple-element.13.vrb_ref) | copy-start | bytes 1572868
  76.3 0.7 copy-start.6
  77.0 28.7 %all-to-all-start.1 = ((f32[16,48,128]{2,1,0:T(8,128)}), f32[16,48,128]{2,1,0:T(8,128)}, u32[]{:S(2)}, u32[]{:S(2)}) async-start(f32[16,48,128]{2,1,0:T(8,128)} %get-tuple-element.17), calls=%async_computation.1 | async-start | bytes 786432 | tf_op jit(solution)/shard_map/all_to_all | solution.py:191
  105.7 33.2 %copy-start.1 = (f32[8,1,128,4,1,128]{5,4,3,2,1,0:T(1,128)S(1)}, f32[8,1,128,4,1,128]{5,4,3,2,1,0:T(1,128)}, u32[]{:S(2)}) copy-start(f32[8,1,128,4,1,128]{5,4,3,2,1,0:T(1,128)} %param.3) | copy-start | bytes 6291460
  105.8 33.1 %copy-start.3 = (f32[1024,128]{1,0:T(8,128)S(1)}, f32[1024,128]{1,0:T(8,128)}, u32[]{:S(2)}) copy-start(f32[1024,128]{1,0:T(8,128)} %copy-done.2) | copy-start | bytes 1572868
  105.8 33.1 %copy-start.5 = (f32[1024,128]{1,0:T(8,128)S(1)}, f32[1024,128]{1,0:T(8,128)}, u32[]{:S(2)}) copy-start(f32[1024,128]{1,0:T(8,128)} %copy-done.4) | copy-start | bytes 1572868
  105.8 33.1 %copy-start.7 = (f32[512,128]{1,0:T(8,128)S(1)}, f32[512,128]{1,0:T(8,128)}, u32[]{:S(2)}) copy-start(f32[512,128]{1,0:T(8,128)} %copy-done.6) | copy-start | bytes 786436
  105.8 33.1 %copy-start.8 = (f32[2,96,96]{2,1,0:T(8,128)S(1)}, f32[2,96,96]{2,1,0:T(8,128)}, u32[]{:S(2)}) copy-start(f32[2,96,96]{2,1,0:T(8,128)} %t_ref.1) | copy-start | bytes 221188

commit v3 on v2

--- a/solution.py
+++ b/solution.py
@@ -26,15 +26,40 @@
     )
 
 
-def call(kernel, outs, scratch, flops, *args):
+def parts(x):
+    high = x.astype(jnp.bfloat16)
+    return high, (x - high.astype(jnp.float32)).astype(jnp.bfloat16)
+
+
+def left_parts(x):
+    high, low = parts(x)
+    return jnp.concatenate([high, low, high], axis=1)
+
+
+def right_parts(x):
+    high, low = parts(x)
+    return jnp.concatenate([high, high, low], axis=0)
+
+
+def plain(a, b):
+    return lax.dot_general(
+        a, b, (((1,), (0,)), ((), ())), preferred_element_type=jnp.float32
+    )
+
+
+HBM = pl.BlockSpec(memory_space=pltpu.HBM)
+VMEM = pl.BlockSpec(memory_space=pltpu.VMEM)
+
+
+def call(kernel, outs, scratch, flops, *args, in_hbm=(), out_hbm=()):
     shapes = [jax.ShapeDtypeStruct(s, jnp.float32) for s in outs]
     moved = sum(x.size for x in list(args) + shapes) * 4
     return pl.pallas_call(
         kernel,
         out_shape=shapes,
-        in_specs=[pl.BlockSpec(memory_space=pltpu.VMEM)] * len(args),
-        out_specs=[pl.BlockSpec(memory_space=pltpu.VMEM)] * len(outs),
-        scratch_shapes=[pltpu.VMEM(s, jnp.float32) for s in scratch],
+        in_specs=[HBM if k in in_hbm else VMEM for k in range(len(args))],
+        out_specs=[HBM if k in out_hbm else VMEM for k in range(len(outs))],
+        scratch_shapes=[pltpu.VMEM(s, jnp.float32) if isinstance(s, tuple) else s for s in scratch],
         compiler_params=pltpu.CompilerParams(vmem_limit_bytes=40 * 1024 * 1024),
         cost_estimate=pl.CostEstimate(flops=flops, bytes_accessed=moved, transcendentals=0),
     )(*args)
@@ -52,7 +77,18 @@
     out_ref[...] = jnp.concatenate(parts, axis=0)
 
 
-def image_kernel(a_ref, g_ref, own_ref, send_ref, va_ref, vb_ref):
+def fetch(hbm_ref, a_ref, sem, pieces):
+    rows = a_ref.shape[0] // pieces
+    copies = []
+    for k in range(pieces):
+        at = pl.ds(k * rows, rows)
+        copies.append(pltpu.make_async_copy(hbm_ref.at[at, :], a_ref.at[at, :], sem.at[k]))
+        copies[-1].start()
+    return copies
+
+
+def image_kernel(hbm_ref, g_ref, own_ref, send_ref, va_ref, vb_ref, a_ref, sem):
+    copies = fetch(hbm_ref, a_ref, sem, 4)
     for x in range(XS):
         for j in range(4):
             for h in range(2):
@@ -70,10 +106,12 @@
                     at = (2 * j + h) * 128 + x * 64 + r
                     vb_ref[pl.ds(at, 16, stride=4), :] = both
                     vb_ref[pl.ds(at + 512, 16, stride=4), :] = pltpu.roll(both, 64, 1)
-    v = jnp.concatenate([va_ref[...], vb_ref[:, :64]], axis=1)
+    v = left_parts(jnp.concatenate([va_ref[...], vb_ref[:, :64]], axis=1).T)
+    for copy in copies:
+        copy.wait()
     for half in range(2):
         tiles = [a_ref[pl.ds(2 * half + t, 1024, stride=4), :] for t in range(2)]
-        q = dot(v, jnp.concatenate(tiles, axis=1), 0, 0)
+        q = plain(v, right_parts(jnp.concatenate(tiles, axis=1)))
         for t in range(2):
             j = 2 * half + t
             for kk in range(12):
@@ -129,18 +167,53 @@
 
 
 def update_kernel(
-    a_ref, vra_ref, vrb_ref, vca_ref, vcb_ref, y_ref, r_ref, t_ref, out_ref, yr_ref, yc_ref
+    hbm_ref, vra_ref, vrb_ref, vca_ref, vcb_ref, y_ref, r_ref, t_ref, to_ref,
+    a_ref, out_ref, yr_ref, yc_ref, left_ref, sem, out_sem,
 ):
+    copies = fetch(hbm_ref, a_ref, sem, 4)
+
     def both(start):
         here = r_ref[pl.ds(start, 16, stride=2 * BLOCK), :]
         return here + r_ref[pl.ds(start + BLOCK, 16, stride=2 * BLOCK), :]
 
+    def mul(a, b):
+        return plain(left_parts(a), right_parts(b))
+
     wide = [both(48 + k) for k in range(12)]
     low = [both(60 + k) for k in range(6)]
+    h11 = jnp.concatenate(wide[:6], axis=0)[:, :W]
     h_a = jnp.concatenate(wide, axis=0)
     h_b = jnp.concatenate([x[:, :64] for x in low] + [x[:, 64:] for x in low], axis=0)
-    ht = jnp.concatenate([h_a, h_b], axis=1)
+    ht = jnp.concatenate([h_a[:, W:], h_b], axis=1)
+    h12 = ht[:W]
+    h22 = ht[W:]
     g = jnp.concatenate([both(66 + k) for k in range(6)], axis=0)[:, :W]
+    t1 = t_ref[0]
+    t2 = t_ref[1]
+    t1t = t1.T
+    tg = mul(t1, g)
+    inner = h12 - 0.5 * mul(h11, tg)
+    shift1 = 0.5 * mul(t1t, mul(h11, t1))
+    crossed = mul(t1t, inner)
+    fold = mul(tg.T, inner)
+    second = h22 - fold - fold.T
+    shift2 = 0.5 * mul(t2.T, mul(second, t2))
+    corner = mul(crossed, t2) - mul(shift1, mul(g, t2))
+    none = jnp.zeros((W, W), jnp.float32)
+    left = jnp.concatenate(
+        [
+            jnp.concatenate([t1, -mul(tg, t2)], axis=1),
+            jnp.concatenate([none, t2], axis=1),
+        ],
+        axis=0,
+    )
+    sym = jnp.concatenate(
+        [
+            jnp.concatenate([shift1 + shift1.T, corner], axis=1),
+            jnp.concatenate([corner.T, shift2 + shift2.T], axis=1),
+        ],
+        axis=0,
+    )
     for k in range(12):
         for j in range(4):
             for x in range(XS):
@@ -151,40 +224,30 @@
             yc_ref[k * 16 : k * 16 + 16, j * 128 : j * 128 + 128] = y_ref[
                 pl.ds(k * 4 + j, 16, stride=SLICE), :
             ]
-    t1 = t_ref[0]
-    t2 = t_ref[1]
-    shift1 = 0.5 * dot(t1, dot(ht[:W, :W], t1), 0, 0)
-    crossed = dot(t1, ht[:W, W:], 0, 0) - dot(shift1, g, 0, 0)
-    fold = dot(g, crossed, 0, 0)
-    second = ht[W:, W:] - fold - fold.T
-    shift2 = 0.5 * dot(t2, dot(second, t2), 0, 0)
-    gt = dot(g, t2)
-    corner = dot(crossed, t2) - dot(shift1, gt)
-    none = jnp.zeros((W, W), jnp.float32)
-    left = jnp.concatenate(
-        [
-            jnp.concatenate([t1, -dot(t1, gt)], axis=1),
-            jnp.concatenate([none, t2], axis=1),
-        ],
-        axis=0,
-    )
-    sym = jnp.concatenate(
-        [
-            jnp.concatenate([shift1 + shift1.T, corner], axis=1),
-            jnp.concatenate([corner.T, shift2 + shift2.T], axis=1),
-        ],
-        axis=0,
-    )
-    vc = jnp.concatenate([vca_ref[...], vcb_ref[:, :64]], axis=1)
-    m1 = dot(left, yc_ref[...], 0, 0) - dot(sym, vc, 1, 1)
-    m2 = dot(left, vc, 1, 1)
-    for i in range(8):
-        at = i * 128
-        vr = jnp.concatenate([vra_ref[at : at + 128, :], vrb_ref[at : at + 128, :64]], axis=1)
-        change = dot(vr, m1) + dot(yr_ref[:, at : at + 128], m2, 0, 0)
+    for i in range(4):
+        at = slice(i * 256, i * 256 + 256)
+        rows = jnp.concatenate(
+            [vra_ref[at, :], vrb_ref[at, :64], yr_ref[:, at].T], axis=1
+        )
+        left_ref[at, :] = left_parts(rows)
+    vc = jnp.concatenate([vca_ref[...], vcb_ref[:, :64]], axis=1).T
+    m1 = mul(left.T, yc_ref[...]) - mul(sym, vc)
+    m2 = mul(left, vc)
+    right = right_parts(jnp.concatenate([m1, m2], axis=0))
+    for copy in copies:
+        copy.wait()
+    outs = []
+    for i in range(4):
+        at = i * 256
+        change = plain(left_ref[at : at + 256, :], right)
         for j in range(4):
-            where = pl.ds(at * 4 + j, 128, stride=4)
+            where = pl.ds(at * 4 + j, 256, stride=4)
             out_ref[where, :] = a_ref[where, :] - change[:, j * 128 : j * 128 + 128]
+        part = pl.ds(at * 4, 1024)
+        outs.append(pltpu.make_async_copy(out_ref.at[part, :], to_ref.at[part, :], out_sem.at[i]))
+        outs[-1].start()
+    for copy in outs:
+        copy.wait()
 
 
 def spread(array, axes):
@@ -192,7 +255,7 @@
 
 
 def shards(matrix, vectors, factors):
-    blocks = matrix.reshape(-1, LANES)
+    blocks = pltpu.with_memory_space_constraint(matrix.reshape(-1, LANES), pltpu.HBM)
     every = [(p, x, z) for p in range(ROWS) for x in range(XS) for z in range(ZS)]
     number = {at: k for k, at in enumerate(every)}
     same = [(number[p, x, z], number[z, x, p]) for p, x, z in every]
@@ -206,11 +269,12 @@
     image, vra, vrb = call(
         image_kernel,
         [(ROWS * 96, LANES), (1024, LANES), (1024, LANES)],
-        [],
+        [(4096, LANES), pltpu.SemaphoreType.DMA((4,))],
         2 * 1024 * 512 * 192,
         blocks,
         gathered,
         own,
+        in_hbm=(0,),
     )
     image = spread(image.reshape(ROWS, 96, LANES), "row").reshape(-1, LANES)
     block, mine, vca, vcb = call(
@@ -227,7 +291,15 @@
     (out,) = call(
         update_kernel,
         [(4096, LANES)],
-        [(192, 1024), (192, 512)],
+        [
+            (4096, LANES),
+            (4096, LANES),
+            (192, 1024),
+            (192, 512),
+            pltpu.VMEM((1024, 1152), jnp.bfloat16),
+            pltpu.SemaphoreType.DMA((4,)),
+            pltpu.SemaphoreType.DMA((4,)),
+        ],
         2 * 1024 * 512 * 384,
         blocks,
         vra,
@@ -237,6 +309,8 @@
         y_cols,
         y_rows,
         factors,
+        in_hbm=(0,),
+        out_hbm=(0,),
     )
     return out.reshape(matrix.shape)
 

time: 148 us -> 143 us (0.966)
  local copies, waits for them, and re-layouts: 3.1 us -> 0.76 us
  Pallas kernels: 12.8 us -> 10.7 us
    unnamed x20 -> x4, local copies, waits for them, and re-layouts: 3.1 us -> 0.76 us
    pallas_call x5, Pallas kernels: 12.8 us -> 10.7 us  [call(): pl.pallas_call(kernel, out_shape=shapes, in_specs=[HBM if k in in_hbm els...]
where the time goes in v3:
time: 143 us
  blocking collectives  121 us (85%)
  Pallas kernels  10.7 us (7%)
  starting transfers between devices  9.82 us (7%)
    all_to_all x2, blocking collectives, spread(): return lax.all_to_all(array, axes, split_axis=0, concat_axis=0, tiled=True)  62.2 us
    all_gather x1, blocking collectives, shards(): lax.all_gather(pair.reshape(2 * SLICE, LANES), 'z', axis=0, tiled=True)  30 us
    all_gather x1, blocking collectives, shards(): block = lax.all_gather(block, 'z')  23.7 us
    pallas_call x5, Pallas kernels, call(): pl.pallas_call(kernel, out_shape=shapes, in_specs=[HBM if k in in_hbm els...  10.7 us
    ppermute x1, starting transfers between devices, shards(): own = lax.ppermute(own.reshape(SLICE, LANES), whole, same)  5.49 us
    all_gather x1, blocking collectives, shards(): pair = lax.all_gather(packed, 'xh')  5.44 us
    all_to_all x1, starting transfers between devices, spread(): return lax.all_to_all(array, axes, split_axis=0, concat_axis=0, tiled=True)  4.33 us
  transfers between devices with their start and end apart: 2, of which 0 were waited for; matrix products, arithmetic and copies ran while one was open for 0% of the time, Pallas kernels for 0%

profile of v3, /device:TPU:1, one launch (start us, length us, event | category | flops | bytes accessed | tf_op | source)
XLA Modules:
  0.0 142.7 jit_solution(8228169941660038870)
XLA Ops:
  0.0 0.0 copy-start.1
  0.0 0.8 copy-done.1
  0.8 0.1 shard_map.37
  0.8 5.4 %all-gather = f32[96,128]{1,0:T(8,128)S(1)} all-gather(f32[48,128]{1,0:T(8,128)S(1)} %shard_map.37), channel_id=2, replica_groups=mesh['row'=16,'xh'=2,'z'=16] {'xh'}, dimensions={0}, use_global_device_ids=true | all-gather | bytes 73728 | tf_op jit(solution)/shard_map/all_gather | solution.py:265
  6.3 5.5 %collective-permute-start = (f32[48,128]{1,0:T(8,128)S(1)}, f32[48,128]{1,0:T(8,128)S(1)}, u32[]{:S(2)}, u32[]{:S(2)}) collective-permute-start(f32[48,128]{1,0:T(8,128)S(1)} %bitcast.21), channel_id=1, source_target_pairs={{0,0},{1,32},{2,64},{3,96},{4,128},{5,160},{6,192},{7,224},{8,256}... | collective-permute-start | bytes 73736 | tf_op jit(solution)/shard_map/ppermute | solution.py:267
  11.8 30.0 %all_gather.17.g_ref = f32[1536,128]{1,0:T(8,128)S(1)} all-gather(f32[96,128]{1,0:T(8,128)S(1)} %all-gather), channel_id=1, replica_groups=mesh['row'=16,'xh'=2,'z'=16] {'z'}, dimensions={0}, use_global_device_ids=true | all-gather | bytes 835584 | tf_op jit(solution)/shard_map/all_gather | solution.py:268
  41.7 0.0 collective-permute-done.own_ref
  41.7 3.1 %shard_map.38 = (f32[1536,128]{1,0:T(8,128)S(1)}, f32[1024,128]{1,0:T(8,128)S(1)}, f32[1024,128]{1,0:T(8,128)S(1)}) custom-call(f32[4096,128]{1,0:T(8,128)} %bitcast.18, f32[1536,128]{1,0:T(8,128)S(1)} %all_gather.17.g_ref, f32[48,128]{1,0:T(8,128)S(1)} %collective-permute-done.own_ref), custom_call_target="tpu_custom_call" | custom-call | flops 201326592 | bytes 4743168 | tf_op jit(solution)/shard_map/pallas_call | solution.py:57
  44.9 29.5 %all_to_all.15 = f32[16,96,128]{2,1,0:T(8,128)S(1)} all-to-all(f32[16,96,128]{2,1,0:T(8,128)S(1)} %bitcast.16), channel_id=1, replica_groups=mesh['row'=16,'xh'=2,'z'=16] {'row'}, dimensions={0} | all-to-all | bytes 1572864 | tf_op jit(solution)/shard_map/all_to_all | solution.py:254
  74.3 1.3 shard_map.39
  75.6 4.3 %all-to-all-start.1 = ((f32[16,48,128]{2,1,0:T(8,128)}), f32[16,48,128]{2,1,0:T(8,128)S(1)}, u32[]{:S(2)}, u32[]{:S(2)}) async-start(f32[16,48,128]{2,1,0:T(8,128)} %get-tuple-element.17), calls=%async_computation.1 | async-start | bytes 786432 | tf_op jit(solution)/shard_map/all_to_all | solution.py:254
  79.9 23.7 %all-gather.1 = f32[1152,128]{1,0:T(8,128)S(1)} all-gather(f32[72,128]{1,0:T(8,128)S(1)} %get-tuple-element.18), channel_id=3, replica_groups=mesh['row'=16,'xh'=2,'z'=16] {'z'}, dimensions={0}, use_global_device_ids=true | all-gather | bytes 626688 | tf_op jit(solution)/shard_map/all_gather | solution.py:288
  103.6 0.0 copy-start
  103.6 0.1 shard_map.40
  103.7 0.0 all-to-all-done.1
  103.7 32.7 %all_to_all.16 = f32[32,72,128]{2,1,0:T(8,128)S(1)} all-to-all(f32[32,72,128]{2,1,0:T(8,128)S(1)} %shard_map.40), channel_id=1, replica_groups=mesh['row'=16,'xh'=2,'z'=16] {'row','xh'}, dimensions={0} | all-to-all | bytes 2359296 | tf_op jit(solution)/shard_map/all_to_all | solution.py:254
  136.4 0.0 copy-done
  136.5 6.2 %shard_map.41 = f32[4096,128]{1,0:T(8,128)} custom-call(f32[4096,128]{1,0:T(8,128)} %bitcast.19, f32[1024,128]{1,0:T(8,128)S(1)} %get-tuple-element.12.vra_ref, f32[1024,128]{1,0:T(8,128)S(1)} %get-tuple-element.13.vrb_ref, f32[512,128]{1,0:T(8,128)S(1)} %get-tuple-element.15.vca_ref, f32[512,128]{1,0:T(8,128)S(1)} %get-tuple-element.16.vcb_ref, ...), custom_call_target="tpu_custom_call" | custom-call | flops 402653184 | bytes 7413760 | tf_op jit(solution)/shard_map/pallas_call | solution.py:57
  (1 shorter events, 0.0 us)
Async XLA Ops:
  0.0 0.8 copy-start.1
  6.3 35.5 %collective-permute-start = (f32[48,128]{1,0:T(8,128)S(1)}, f32[48,128]{1,0:T(8,128)S(1)}, u32[]{:S(2)}, u32[]{:S(2)}) collective-permute-start(f32[48,128]{1,0:T(8,128)S(1)} %bitcast.21), channel_id=1, source_target_pairs={{0,0},{1,32},{2,64},{3,96},{4,128},{5,160},{6,192},{7,224},{8,256}... | collective-permute-start | bytes 73736 | tf_op jit(solution)/shard_map/ppermute | solution.py:267
  75.6 28.1 %all-to-all-start.1 = ((f32[16,48,128]{2,1,0:T(8,128)}), f32[16,48,128]{2,1,0:T(8,128)S(1)}, u32[]{:S(2)}, u32[]{:S(2)}) async-start(f32[16,48,128]{2,1,0:T(8,128)} %get-tuple-element.17), calls=%async_computation.1 | async-start | bytes 786432 | tf_op jit(solution)/shard_map/all_to_all | solution.py:254
  103.6 32.8 %copy-start = (f32[2,96,96]{2,1,0:T(8,128)S(1)}, f32[2,96,96]{2,1,0:T(8,128)}, u32[]{:S(2)}) copy-start(f32[2,96,96]{2,1,0:T(8,128)} %t_ref.1) | copy-start | bytes 221188

commit v4 on v3

--- a/solution.py
+++ b/solution.py
@@ -13,7 +13,9 @@
 LANES = 128
 SLICE = 48
 PART = 24
-BLOCK = 72
+BLOCK = 64
+MINE = 56
+SEND = 104
 
 
 def dot(a, b, ca=1, cb=0):
@@ -88,7 +90,7 @@
 
 
 def image_kernel(hbm_ref, g_ref, own_ref, send_ref, va_ref, vb_ref, a_ref, sem):
-    copies = fetch(hbm_ref, a_ref, sem, 4)
+    copies = fetch(hbm_ref, a_ref, sem, 8)
     for x in range(XS):
         for j in range(4):
             for h in range(2):
@@ -106,64 +108,73 @@
                     at = (2 * j + h) * 128 + x * 64 + r
                     vb_ref[pl.ds(at, 16, stride=4), :] = both
                     vb_ref[pl.ds(at + 512, 16, stride=4), :] = pltpu.roll(both, 64, 1)
-    v = left_parts(jnp.concatenate([va_ref[...], vb_ref[:, :64]], axis=1).T)
-    for copy in copies:
-        copy.wait()
-    for half in range(2):
-        tiles = [a_ref[pl.ds(2 * half + t, 1024, stride=4), :] for t in range(2)]
-        q = plain(v, right_parts(jnp.concatenate(tiles, axis=1)))
-        for t in range(2):
-            j = 2 * half + t
-            for kk in range(12):
-                send_ref[pl.ds(kk * 4 + j, 16, stride=2 * SLICE), :] = q[
-                    kk * 16 : kk * 16 + 16, t * 128 : t * 128 + 128
-                ]
+    q = 0.0
+    gram = 0.0
+    for c in range(4):
+        at = slice(c * 256, c * 256 + 256)
+        v = jnp.concatenate([va_ref[at, :], vb_ref[at, :64]], axis=1)
+        left = left_parts(v.T)
+        gram = gram + plain(left[:W], right_parts(v[:, W:]))
+        copies[2 * c].wait()
+        copies[2 * c + 1].wait()
+        tiles = [a_ref[pl.ds(c * 1024 + j, 256, stride=4), :] for j in range(4)]
+        q = q + plain(left, right_parts(jnp.concatenate(tiles, axis=1)))
+    for j in range(4):
+        for kk in range(12):
+            send_ref[pl.ds(kk * 4 + j, 16, stride=SEND), :] = q[
+                kk * 16 : kk * 16 + 16, j * 128 : j * 128 + 128
+            ]
+    gram = jnp.concatenate([gram, jnp.zeros((W, 32), jnp.float32)], axis=1)
+    for k in range(8):
+        rows = gram[k * 16 : k * 16 + 16] if k < 6 else jnp.zeros((16, LANES), jnp.float32)
+        send_ref[pl.ds(SLICE + k, 16, stride=SEND), :] = rows
     own = own_ref[...]
     for k in range(ROWS):
-        send_ref[k * 96 + 48 : k * 96 + 96, :] = own
+        send_ref[k * SEND + MINE : k * SEND + SEND, :] = own
 
 
 def slice_kernel(r_ref, block_ref, y_ref, va_ref, vb_ref, sum_ref):
-    me = lax.axis_index("row")
-    total = r_ref[0:48, :]
+    total = r_ref[0:MINE, :]
     for k in range(1, ROWS):
-        total = total + r_ref[k * 96 : k * 96 + 48, :]
+        total = total + r_ref[k * SEND : k * SEND + MINE, :]
     sum_ref[...] = total
     for x in range(XS):
         for j in range(4):
             for r in range(4):
                 va_ref[pl.ds(j * 128 + x * 64 + r, 16, stride=4), :] = r_ref[
-                    pl.ds(48 + x * 24 + j * 4 + r, 16, stride=96), :
+                    pl.ds(MINE + x * 24 + j * 4 + r, 16, stride=SEND), :
                 ]
         for j in range(2):
             for r in range(4):
-                both = r_ref[pl.ds(64 + x * 24 + j * 4 + r, 16, stride=96), :]
+                both = r_ref[pl.ds(MINE + 16 + x * 24 + j * 4 + r, 16, stride=SEND), :]
                 vb_ref[pl.ds(j * 128 + x * 64 + r, 16, stride=4), :] = both
                 vb_ref[pl.ds((j + 2) * 128 + x * 64 + r, 16, stride=4), :] = pltpu.roll(both, 64, 1)
     v = jnp.concatenate([va_ref[...], vb_ref[:, :64]], axis=1)
     y = jnp.concatenate([sum_ref[pl.ds(j, 12, stride=4), :] for j in range(4)], axis=1)
     ht = dot(y, v)
-    gram = dot(v[:, :W], v[:, W:], 0, 0)
-    at = lax.broadcasted_iota(jnp.int32, (8, W), 0) * 16 + me
-    pick = jnp.where(at == lax.broadcasted_iota(jnp.int32, (8, W), 1), 1.0, 0.0)
-    mine = dot(pick, gram)
-    low = jnp.concatenate([ht[0:6, 128:], ht[6:12, 128:]], axis=1)
-    mine = jnp.concatenate([mine[0:6], jnp.zeros((6, 32), jnp.float32)], axis=1)
-    tail = jnp.concatenate([ht[:, :128], low, mine], axis=0)
-    block_ref[0:48, :] = total
-    block_ref[48:72, :] = tail
+    low = jnp.concatenate([ht[0:6, LANES:], ht[6:12, W : W + 64]], axis=1)
+    end = ht[6:12, W + 64 :]
+    none = jnp.zeros((1, 32), jnp.float32)
+    ends = [
+        jnp.concatenate([end[k : k + 1], end[k + 1 : k + 2], end[k + 2 : k + 3], none], axis=1)
+        for k in (0, 3)
+    ]
+    block_ref[0:48, :] = total[:SLICE]
+    block_ref[48:64, :] = jnp.concatenate(
+        [ht[0:6, :LANES], low] + ends + [jnp.zeros((2, LANES), jnp.float32)], axis=0
+    )
     for k in range(ROWS):
         y_ref[k] = total
 
 
 def turn_kernel(r_ref, out_ref):
-    tail = r_ref[0, 48:72, :]
+    tail = r_ref[0, 48:BLOCK, :]
     for k in range(1, ZS):
-        tail = tail + r_ref[k, 48:72, :]
+        tail = tail + r_ref[k, 48:BLOCK, :]
     for k in range(ROWS):
         for x in range(XS):
             out_ref[2 * k + x, 0:48, :] = r_ref[k, 0:48, :]
-            out_ref[2 * k + x, 48:72, :] = tail
+            out_ref[2 * k + x, 48:BLOCK, :] = tail
 
 
 def update_kernel(
@@ -179,15 +190,17 @@
     def mul(a, b):
         return plain(left_parts(a), right_parts(b))
 
-    wide = [both(48 + k) for k in range(12)]
-    low = [both(60 + k) for k in range(6)]
-    h11 = jnp.concatenate(wide[:6], axis=0)[:, :W]
-    h_a = jnp.concatenate(wide, axis=0)
-    h_b = jnp.concatenate([x[:, :64] for x in low] + [x[:, 64:] for x in low], axis=0)
-    ht = jnp.concatenate([h_a[:, W:], h_b], axis=1)
-    h12 = ht[:W]
-    h22 = ht[W:]
-    g = jnp.concatenate([both(66 + k) for k in range(6)], axis=0)[:, :W]
+    wide = jnp.concatenate([both(48 + k) for k in range(6)], axis=0)
+    low = jnp.concatenate([both(54 + k) for k in range(6)], axis=0)
+    ends = [both(60 + k) for k in range(2)]
+    end = jnp.concatenate(
+        [ends[k // 3][:, k % 3 * 32 : k % 3 * 32 + 32] for k in range(6)], axis=0
+    )
+    h11 = wide[:, :W]
+    h12 = jnp.concatenate([wide[:, W:], low[:, :64]], axis=1)
+    h22 = jnp.concatenate([low[:, 64:], end], axis=1)
+    g = [y_ref[pl.ds(SLICE + k, 16, stride=MINE), :] for k in range(6)]
+    g = jnp.concatenate(g, axis=0)[:, :W]
     t1 = t_ref[0]
     t2 = t_ref[1]
     t1t = t1.T
@@ -222,7 +235,7 @@
                     pl.ds(x * BLOCK + k * 4 + j, 16, stride=2 * BLOCK), :
                 ]
             yc_ref[k * 16 : k * 16 + 16, j * 128 : j * 128 + 128] = y_ref[
-                pl.ds(k * 4 + j, 16, stride=SLICE), :
+                pl.ds(k * 4 + j, 16, stride=MINE), :
             ]
     for i in range(4):
         at = slice(i * 256, i * 256 + 256)
@@ -268,19 +281,19 @@
     gathered = lax.all_gather(pair.reshape(2 * SLICE, LANES), "z", axis=0, tiled=True)
     image, vra, vrb = call(
         image_kernel,
-        [(ROWS * 96, LANES), (1024, LANES), (1024, LANES)],
-        [(4096, LANES), pltpu.SemaphoreType.DMA((4,))],
+        [(ROWS * SEND, LANES), (1024, LANES), (1024, LANES)],
+        [(4096, LANES), pltpu.SemaphoreType.DMA((8,))],
         2 * 1024 * 512 * 192,
         blocks,
         gathered,
         own,
         in_hbm=(0,),
     )
-    image = spread(image.reshape(ROWS, 96, LANES), "row").reshape(-1, LANES)
+    image = spread(image.reshape(ROWS, SEND, LANES), "row").reshape(-1, LANES)
     block, mine, vca, vcb = call(
         slice_kernel,
-        [(BLOCK, LANES), (ROWS, SLICE, LANES), (512, LANES), (512, LANES)],
-        [(SLICE, LANES)],
+        [(BLOCK, LANES), (ROWS, MINE, LANES), (512, LANES), (512, LANES)],
+        [(MINE, LANES)],
         2 * 512 * 192 * 96,
         image,
     )

time: 143 us -> 142 us (level)
    all_to_all x2, blocking collectives: 62.2 us -> 60.7 us  [spread(): return lax.all_to_all(array, axes, split_axis=0, concat_axis=0, tiled=True)]
where the time goes in v4:
time: 142 us; the launch traced here: 141 us
  blocking collectives  120 us (85%)
  Pallas kernels  10.7 us (8%)
  starting transfers between devices  10 us (7%)
    all_to_all x2, blocking collectives, spread(): return lax.all_to_all(array, axes, split_axis=0, concat_axis=0, tiled=True)  60.7 us
    all_gather x1, blocking collectives, shards(): lax.all_gather(pair.reshape(2 * SLICE, LANES), 'z', axis=0, tiled=True)  30 us
    all_gather x1, blocking collectives, shards(): block = lax.all_gather(block, 'z')  23.5 us
    pallas_call x5, Pallas kernels, call(): pl.pallas_call(kernel, out_shape=shapes, in_specs=[HBM if k in in_hbm els...  10.7 us
    ppermute x1, starting transfers between devices, shards(): own = lax.ppermute(own.reshape(SLICE, LANES), whole, same)  5.49 us
    all_gather x1, blocking collectives, shards(): pair = lax.all_gather(packed, 'xh')  5.44 us
    all_to_all x1, starting transfers between devices, spread(): return lax.all_to_all(array, axes, split_axis=0, concat_axis=0, tiled=True)  4.52 us
  transfers between devices with their start and end apart: 2, of which 0 were waited for; matrix products, arithmetic and copies ran while one was open for 0% of the time, Pallas kernels for 0%

profile of v4, /device:TPU:1, one launch (start us, length us, event | category | flops | bytes accessed | tf_op | source)
XLA Modules:
  0.0 141.2 jit_solution(398737905142780284)
XLA Ops:
  0.0 0.0 copy-start.1
  0.0 0.8 copy-done.1
  0.8 0.1 shard_map.37
  0.8 5.4 %all-gather = f32[96,128]{1,0:T(8,128)S(1)} all-gather(f32[48,128]{1,0:T(8,128)S(1)} %shard_map.37), channel_id=2, replica_groups=mesh['row'=16,'xh'=2,'z'=16] {'xh'}, dimensions={0}, use_global_device_ids=true | all-gather | bytes 73728 | tf_op jit(solution)/shard_map/all_gather | solution.py:278
  6.3 5.5 %collective-permute-start = (f32[48,128]{1,0:T(8,128)S(1)}, f32[48,128]{1,0:T(8,128)S(1)}, u32[]{:S(2)}, u32[]{:S(2)}) collective-permute-start(f32[48,128]{1,0:T(8,128)S(1)} %bitcast.21), channel_id=1, source_target_pairs={{0,0},{1,32},{2,64},{3,96},{4,128},{5,160},{6,192},{7,224},{8,256}... | collective-permute-start | bytes 73736 | tf_op jit(solution)/shard_map/ppermute | solution.py:280
  11.8 30.0 %all_gather.17.g_ref = f32[1536,128]{1,0:T(8,128)S(1)} all-gather(f32[96,128]{1,0:T(8,128)S(1)} %all-gather), channel_id=1, replica_groups=mesh['row'=16,'xh'=2,'z'=16] {'z'}, dimensions={0}, use_global_device_ids=true | all-gather | bytes 835584 | tf_op jit(solution)/shard_map/all_gather | solution.py:281
  41.7 0.0 collective-permute-done.own_ref
  41.7 3.1 %shard_map.38 = (f32[1664,128]{1,0:T(8,128)S(1)}, f32[1024,128]{1,0:T(8,128)S(1)}, f32[1024,128]{1,0:T(8,128)S(1)}) custom-call(f32[4096,128]{1,0:T(8,128)} %bitcast.18, f32[1536,128]{1,0:T(8,128)S(1)} %all_gather.17.g_ref, f32[48,128]{1,0:T(8,128)S(1)} %collective-permute-done.own_ref), custom_call_target="tpu_custom_call" | custom-call | flops 201326592 | bytes 4808704 | tf_op jit(solution)/shard_map/pallas_call | solution.py:59
  44.9 30.0 %all_to_all.15 = f32[16,104,128]{2,1,0:T(8,128)S(1)} all-to-all(f32[16,104,128]{2,1,0:T(8,128)S(1)} %bitcast.16), channel_id=1, replica_groups=mesh['row'=16,'xh'=2,'z'=16] {'row'}, dimensions={0} | all-to-all | bytes 1703936 | tf_op jit(solution)/shard_map/all_to_all | solution.py:267
  74.9 1.2 shard_map.39
  76.0 4.5 %all-to-all-start.1 = ((f32[16,56,128]{2,1,0:T(8,128)}), f32[16,56,128]{2,1,0:T(8,128)S(1)}, u32[]{:S(2)}, u32[]{:S(2)}) async-start(f32[16,56,128]{2,1,0:T(8,128)} %get-tuple-element.17), calls=%async_computation.1 | async-start | bytes 917504 | tf_op jit(solution)/shard_map/all_to_all | solution.py:267
  80.5 0.0 copy-start
  80.5 23.5 %all-gather.1 = f32[1024,128]{1,0:T(8,128)S(1)} all-gather(f32[64,128]{1,0:T(8,128)S(1)} %get-tuple-element.18), channel_id=3, replica_groups=mesh['row'=16,'xh'=2,'z'=16] {'z'}, dimensions={0}, use_global_device_ids=true | all-gather | bytes 557056 | tf_op jit(solution)/shard_map/all_gather | solution.py:301
  104.1 0.1 shard_map.40
  104.1 0.0 all-to-all-done.1
  104.1 30.7 %all_to_all.16 = f32[32,64,128]{2,1,0:T(8,128)S(1)} all-to-all(f32[32,64,128]{2,1,0:T(8,128)S(1)} %shard_map.40), channel_id=1, replica_groups=mesh['row'=16,'xh'=2,'z'=16] {'row','xh'}, dimensions={0} | all-to-all | bytes 2097152 | tf_op jit(solution)/shard_map/all_to_all | solution.py:267
  134.9 0.0 copy-done
  134.9 6.3 %shard_map.41 = f32[4096,128]{1,0:T(8,128)} custom-call(f32[4096,128]{1,0:T(8,128)} %bitcast.19, f32[1024,128]{1,0:T(8,128)S(1)} %get-tuple-element.12.vra_ref, f32[1024,128]{1,0:T(8,128)S(1)} %get-tuple-element.13.vrb_ref, f32[512,128]{1,0:T(8,128)S(1)} %get-tuple-element.15.vca_ref, f32[512,128]{1,0:T(8,128)S(1)} %get-tuple-element.16.vcb_ref, ...), custom_call_target="tpu_custom_call" | custom-call | flops 402653184 | bytes 7348224 | tf_op jit(solution)/shard_map/pallas_call | solution.py:59
  (1 shorter events, 0.0 us)
Async XLA Ops:
  0.0 0.8 copy-start.1
  6.3 35.5 %collective-permute-start = (f32[48,128]{1,0:T(8,128)S(1)}, f32[48,128]{1,0:T(8,128)S(1)}, u32[]{:S(2)}, u32[]{:S(2)}) collective-permute-start(f32[48,128]{1,0:T(8,128)S(1)} %bitcast.21), channel_id=1, source_target_pairs={{0,0},{1,32},{2,64},{3,96},{4,128},{5,160},{6,192},{7,224},{8,256}... | collective-permute-start | bytes 73736 | tf_op jit(solution)/shard_map/ppermute | solution.py:280
  76.0 28.1 %all-to-all-start.1 = ((f32[16,56,128]{2,1,0:T(8,128)}), f32[16,56,128]{2,1,0:T(8,128)S(1)}, u32[]{:S(2)}, u32[]{:S(2)}) async-start(f32[16,56,128]{2,1,0:T(8,128)} %get-tuple-element.17), calls=%async_computation.1 | async-start | bytes 917504 | tf_op jit(solution)/shard_map/all_to_all | solution.py:267
  80.5 54.3 %copy-start = (f32[2,96,96]{2,1,0:T(8,128)S(1)}, f32[2,96,96]{2,1,0:T(8,128)}, u32[]{:S(2)}) copy-start(f32[2,96,96]{2,1,0:T(8,128)} %t_ref.1) | copy-start | bytes 221188

commit v5 on v4

--- a/solution.py
+++ b/solution.py
@@ -49,14 +49,28 @@
     )
 
 
+def times(a, b):
+    return plain(a[0], b[0]) + plain(a[1], b[0]) + plain(a[0], b[1])
+
+
+def mul(a, b):
+    return times(parts(a), parts(b))
+
+
 HBM = pl.BlockSpec(memory_space=pltpu.HBM)
 VMEM = pl.BlockSpec(memory_space=pltpu.VMEM)
 
 
 def call(kernel, outs, scratch, flops, *args, in_hbm=(), out_hbm=()):
-    shapes = [jax.ShapeDtypeStruct(s, jnp.float32) for s in outs]
+    shapes = [
+        jax.ShapeDtypeStruct(s, jnp.float32) if isinstance(s[0], int) else jax.ShapeDtypeStruct(*s)
+        for s in outs
+    ]
     moved = sum(x.size for x in list(args) + shapes) * 4
-    return pl.pallas_call(
+    shapes = [
+        pltpu.HBM(x.shape, x.dtype) if k in out_hbm else x for k, x in enumerate(shapes)
+    ]
+    return list(pl.pallas_call(
         kernel,
         out_shape=shapes,
         in_specs=[HBM if k in in_hbm else VMEM for k in range(len(args))],
@@ -64,7 +78,7 @@
         scratch_shapes=[pltpu.VMEM(s, jnp.float32) if isinstance(s, tuple) else s for s in scratch],
         compiler_params=pltpu.CompilerParams(vmem_limit_bytes=40 * 1024 * 1024),
         cost_estimate=pl.CostEstimate(flops=flops, bytes_accessed=moved, transcendentals=0),
-    )(*args)
+    )(*args))
 
 
 def pack_kernel(v_ref, out_ref):
@@ -86,6 +100,16 @@
         at = pl.ds(k * rows, rows)
         copies.append(pltpu.make_async_copy(hbm_ref.at[at, :], a_ref.at[at, :], sem.at[k]))
         copies[-1].start()
+    return copies
+
+
+def move(sources, targets, sem):
+    copies = [
+        pltpu.make_async_copy(source, target, sem.at[k])
+        for k, (source, target) in enumerate(zip(sources, targets))
+    ]
+    for copy in copies:
+        copy.start()
     return copies
 
 
@@ -133,7 +157,7 @@
         send_ref[k * SEND + MINE : k * SEND + SEND, :] = own
 
 
-def slice_kernel(r_ref, block_ref, y_ref, va_ref, vb_ref, sum_ref):
+def slice_kernel(r_ref, block_ref, y_ref, to_a, to_b, sum_ref, va_ref, vb_ref, sem):
     total = r_ref[0:MINE, :]
     for k in range(1, ROWS):
         total = total + r_ref[k * SEND : k * SEND + MINE, :]
@@ -149,6 +173,7 @@
                 both = r_ref[pl.ds(MINE + 16 + x * 24 + j * 4 + r, 16, stride=SEND), :]
                 vb_ref[pl.ds(j * 128 + x * 64 + r, 16, stride=4), :] = both
                 vb_ref[pl.ds((j + 2) * 128 + x * 64 + r, 16, stride=4), :] = pltpu.roll(both, 64, 1)
+    copies = move((va_ref, vb_ref), (to_a, to_b), sem)
     v = jnp.concatenate([va_ref[...], vb_ref[:, :64]], axis=1)
     y = jnp.concatenate([sum_ref[pl.ds(j, 12, stride=4), :] for j in range(4)], axis=1)
     ht = dot(y, v)
@@ -165,6 +190,8 @@
     )
     for k in range(ROWS):
         y_ref[k] = total
+    for copy in copies:
+        copy.wait()
 
 
 def turn_kernel(r_ref, out_ref):
@@ -177,41 +204,23 @@
             out_ref[2 * k + x, 48:BLOCK, :] = tail
 
 
-def update_kernel(
-    hbm_ref, vra_ref, vrb_ref, vca_ref, vcb_ref, y_ref, r_ref, t_ref, to_ref,
-    a_ref, out_ref, yr_ref, yc_ref, left_ref, sem, out_sem,
+def ready_kernel(
+    from_a, from_b, y_ref, t_ref, to_1, to_2, to_high, to_low, tg_ref, gt_ref,
+    yc_ref, vca_ref, vcb_ref, m1_ref, m2_ref, high_ref, low_ref, sem, out_sem,
 ):
-    copies = fetch(hbm_ref, a_ref, sem, 4)
-
-    def both(start):
-        here = r_ref[pl.ds(start, 16, stride=2 * BLOCK), :]
-        return here + r_ref[pl.ds(start + BLOCK, 16, stride=2 * BLOCK), :]
-
-    def mul(a, b):
-        return plain(left_parts(a), right_parts(b))
-
-    wide = jnp.concatenate([both(48 + k) for k in range(6)], axis=0)
-    low = jnp.concatenate([both(54 + k) for k in range(6)], axis=0)
-    ends = [both(60 + k) for k in range(2)]
-    end = jnp.concatenate(
-        [ends[k // 3][:, k % 3 * 32 : k % 3 * 32 + 32] for k in range(6)], axis=0
-    )
-    h11 = wide[:, :W]
-    h12 = jnp.concatenate([wide[:, W:], low[:, :64]], axis=1)
-    h22 = jnp.concatenate([low[:, 64:], end], axis=1)
+    copies = move((from_a, from_b), (vca_ref, vcb_ref), sem)
+    for k in range(12):
+        for j in range(4):
+            yc_ref[k * 16 : k * 16 + 16, j * 128 : j * 128 + 128] = y_ref[
+                pl.ds(k * 4 + j, 16, stride=MINE), :
+            ]
     g = [y_ref[pl.ds(SLICE + k, 16, stride=MINE), :] for k in range(6)]
     g = jnp.concatenate(g, axis=0)[:, :W]
     t1 = t_ref[0]
     t2 = t_ref[1]
-    t1t = t1.T
     tg = mul(t1, g)
-    inner = h12 - 0.5 * mul(h11, tg)
-    shift1 = 0.5 * mul(t1t, mul(h11, t1))
-    crossed = mul(t1t, inner)
-    fold = mul(tg.T, inner)
-    second = h22 - fold - fold.T
-    shift2 = 0.5 * mul(t2.T, mul(second, t2))
-    corner = mul(crossed, t2) - mul(shift1, mul(g, t2))
+    tg_ref[...] = tg
+    gt_ref[...] = mul(g, t2)
     none = jnp.zeros((W, W), jnp.float32)
     left = jnp.concatenate(
         [
@@ -220,6 +229,50 @@
         ],
         axis=0,
     )
+    for copy in copies:
+        copy.wait()
+    vc = parts(jnp.concatenate([vca_ref[...], vcb_ref[:, :64]], axis=1).T)
+    high_ref[...], low_ref[...] = vc
+    m1_ref[...] = mul(left.T, yc_ref[...])
+    m2_ref[...] = times(parts(left), vc)
+    own = (m1_ref, m2_ref, high_ref, low_ref)
+    for copy in move(own, (to_1, to_2, to_high, to_low), out_sem):
+        copy.wait()
+
+
+def update_kernel(
+    hbm_ref, vra_ref, vrb_ref, from_1, from_2, from_high, from_low, tg_ref, gt_ref, r_ref, t_ref,
+    to_ref, a_ref, out_ref, yr_ref, left_ref, m1_ref, m2_ref, high_ref, low_ref,
+    sem, out_sem, in_sem,
+):
+    own = (high_ref, low_ref, m1_ref, m2_ref)
+    given = move((from_high, from_low, from_1, from_2), own, in_sem)
+    copies = fetch(hbm_ref, a_ref, sem, 4)
+
+    def both(start):
+        here = r_ref[pl.ds(start, 16, stride=2 * BLOCK), :]
+        return here + r_ref[pl.ds(start + BLOCK, 16, stride=2 * BLOCK), :]
+
+    wide = jnp.concatenate([both(48 + k) for k in range(6)], axis=0)
+    low = jnp.concatenate([both(54 + k) for k in range(6)], axis=0)
+    ends = [both(60 + k) for k in range(2)]
+    end = jnp.concatenate(
+        [ends[k // 3][:, k % 3 * 32 : k % 3 * 32 + 32] for k in range(6)], axis=0
+    )
+    h11 = wide[:, :W]
+    h12 = jnp.concatenate([wide[:, W:], low[:, :64]], axis=1)
+    h22 = jnp.concatenate([low[:, 64:], end], axis=1)
+    t1 = t_ref[0]
+    t2 = t_ref[1]
+    t1t = t1.T
+    tg = tg_ref[...]
+    inner = h12 - 0.5 * mul(h11, tg)
+    shift1 = 0.5 * mul(t1t, mul(h11, t1))
+    crossed = mul(t1t, inner)
+    fold = mul(tg.T, inner)
+    second = h22 - fold - fold.T
+    shift2 = 0.5 * mul(t2.T, mul(second, t2))
+    corner = mul(crossed, t2) - mul(shift1, gt_ref[...])
     sym = jnp.concatenate(
         [
             jnp.concatenate([shift1 + shift1.T, corner], axis=1),
@@ -234,19 +287,18 @@
                 yr_ref[k * 16 : k * 16 + 16, i * 128 : i * 128 + 128] = r_ref[
                     pl.ds(x * BLOCK + k * 4 + j, 16, stride=2 * BLOCK), :
                 ]
-            yc_ref[k * 16 : k * 16 + 16, j * 128 : j * 128 + 128] = y_ref[
-                pl.ds(k * 4 + j, 16, stride=MINE), :
-            ]
     for i in range(4):
         at = slice(i * 256, i * 256 + 256)
+        y = yr_ref[:, at].T
         rows = jnp.concatenate(
-            [vra_ref[at, :], vrb_ref[at, :64], yr_ref[:, at].T], axis=1
+            [vra_ref[at, :], y[:, :128], vrb_ref[at, :64], y[:, 128:]], axis=1
         )
         left_ref[at, :] = left_parts(rows)
-    vc = jnp.concatenate([vca_ref[...], vcb_ref[:, :64]], axis=1).T
-    m1 = mul(left.T, yc_ref[...]) - mul(sym, vc)
-    m2 = mul(left, vc)
-    right = right_parts(jnp.concatenate([m1, m2], axis=0))
+    for copy in given:
+        copy.wait()
+    m1 = m1_ref[...] - times(parts(sym), (high_ref[...], low_ref[...]))
+    m2 = m2_ref[...]
+    right = right_parts(jnp.concatenate([m1[:128], m2[:128], m1[128:], m2[128:]], axis=0))
     for copy in copies:
         copy.wait()
     outs = []
@@ -293,14 +345,42 @@
     block, mine, vca, vcb = call(
         slice_kernel,
         [(BLOCK, LANES), (ROWS, MINE, LANES), (512, LANES), (512, LANES)],
-        [(MINE, LANES)],
+        [(MINE, LANES), (512, LANES), (512, LANES), pltpu.SemaphoreType.DMA((2,))],
         2 * 512 * 192 * 96,
         image,
+        out_hbm=(2, 3),
     )
     y_cols = spread(mine, "row").reshape(-1, LANES)
     block = lax.all_gather(block, "z")
     (block,) = call(turn_kernel, [(2 * ROWS, BLOCK, LANES)], [], 0, block)
     y_rows = spread(block, ("row", "xh")).reshape(-1, LANES)
+    vca, vcb = (pltpu.with_memory_space_constraint(x, pltpu.HBM) for x in (vca, vcb))
+    small = [(192, 512), (192, 512)]
+    small += [((192, 512), jnp.bfloat16)] * 2 + [(W, W)] * 2
+    half = pltpu.VMEM((192, 512), jnp.bfloat16)
+    ready = call(
+        ready_kernel,
+        small,
+        [
+            (192, 512),
+            (512, LANES),
+            (512, LANES),
+            (192, 512),
+            (192, 512),
+            half,
+            half,
+            pltpu.SemaphoreType.DMA((2,)),
+            pltpu.SemaphoreType.DMA((4,)),
+        ],
+        12 * 192 * 192 * 512,
+        vca,
+        vcb,
+        y_cols,
+        factors,
+        in_hbm=(0, 1),
+        out_hbm=(0, 1, 2, 3),
+    )
+    ready[:4] = [pltpu.with_memory_space_constraint(x, pltpu.HBM) for x in ready[:4]]
     (out,) = call(
         update_kernel,
         [(4096, LANES)],
@@ -308,8 +388,12 @@
             (4096, LANES),
             (4096, LANES),
             (192, 1024),
+            pltpu.VMEM((1024, 1152), jnp.bfloat16),
             (192, 512),
-            pltpu.VMEM((1024, 1152), jnp.bfloat16),
+            (192, 512),
+            half,
+            half,
+            pltpu.SemaphoreType.DMA((4,)),
             pltpu.SemaphoreType.DMA((4,)),
             pltpu.SemaphoreType.DMA((4,)),
         ],
@@ -317,12 +401,10 @@
         blocks,
         vra,
         vrb,
-        vca,
-        vcb,
-        y_cols,
+        *ready,
         y_rows,
         factors,
-        in_hbm=(0,),
+        in_hbm=(0, 3, 4, 5, 6),
         out_hbm=(0,),
     )
     return out.reshape(matrix.shape)

time: 142 us -> 143 us (level)
  blocking collectives: 120 us -> 88.9 us
  waiting for transfers between devices: 0.01 us -> 14.1 us
  starting transfers between devices: 10 us -> 24 us
  Pallas kernels: 10.7 us -> 14.4 us
    all_to_all x2 -> x1, blocking collectives: 60.7 us -> 30 us  [spread(): return lax.all_to_all(array, axes, split_axis=0, concat_axis=0, tiled=True)]
    all_to_all x1 -> x2, waiting for transfers between devices: 0.01 us -> 14.1 us  [spread(): return lax.all_to_all(array, axes, split_axis=0, concat_axis=0, tiled=True)]
    all_to_all x1 -> x2, starting transfers between devices: 4.52 us -> 18.5 us  [spread(): return lax.all_to_all(array, axes, split_axis=0, concat_axis=0, tiled=True)]
    pallas_call x5 -> x6, Pallas kernels: 10.7 us -> 14.4 us  [call(): pl.pallas_call(kernel, out_shape=shapes, in_specs=[HBM if k in in_hbm els...]
  transfers between devices with their start and end apart: 2 -> 3, of which waited for: 0 -> 1; matrix products, arithmetic and copies ran while one was open for 0% -> 0% of each run, Pallas kernels for 0% -> 3%
where the time goes in v5:
time: 143 us; the launch traced here: 142 us
  blocking collectives  88.9 us (62%)
  starting transfers between devices  24 us (17%)
  Pallas kernels  14.4 us (10%)
  waiting for transfers between devices  14.1 us (10%)
    all_to_all x1, blocking collectives, spread(): return lax.all_to_all(array, axes, split_axis=0, concat_axis=0, tiled=True)  30 us
    all_gather x1, blocking collectives, shards(): lax.all_gather(pair.reshape(2 * SLICE, LANES), 'z', axis=0, tiled=True)  30 us
    all_gather x1, blocking collectives, shards(): block = lax.all_gather(block, 'z')  23.5 us
    all_to_all x2, starting transfers between devices, spread(): return lax.all_to_all(array, axes, split_axis=0, concat_axis=0, tiled=True)  18.5 us
    pallas_call x6, Pallas kernels, call(): pl.pallas_call(kernel, out_shape=shapes, in_specs=[HBM if k in in_hbm els...  14.4 us
    all_to_all x2, waiting for transfers between devices, spread(): return lax.all_to_all(array, axes, split_axis=0, concat_axis=0, tiled=True)  14.1 us
    ppermute x1, starting transfers between devices, shards(): own = lax.ppermute(own.reshape(SLICE, LANES), whole, same)  5.49 us
    all_gather x1, blocking collectives, shards(): pair = lax.all_gather(packed, 'xh')  5.44 us
  transfers between devices with their start and end apart: 3, of which 1 were waited for; matrix products, arithmetic and copies ran while one was open for 0% of the time, Pallas kernels for 3%

profile of v5, /device:TPU:1, one launch (start us, length us, event | category | flops | bytes accessed | tf_op | source)
XLA Modules:
  0.0 142.2 jit_solution(7282179769472560748)
XLA Ops:
  0.0 0.0 copy-start.1
  0.0 0.8 copy-done.1
  0.8 0.1 shard_map.37
  0.8 5.4 %all-gather = f32[96,128]{1,0:T(8,128)S(1)} all-gather(f32[48,128]{1,0:T(8,128)S(1)} %shard_map.37), channel_id=2, replica_groups=mesh['row'=16,'xh'=2,'z'=16] {'xh'}, dimensions={0}, use_global_device_ids=true | all-gather | bytes 73728 | tf_op jit(solution)/shard_map/all_gather | solution.py:330
  6.3 5.5 %collective-permute-start = (f32[48,128]{1,0:T(8,128)S(1)}, f32[48,128]{1,0:T(8,128)S(1)}, u32[]{:S(2)}, u32[]{:S(2)}) collective-permute-start(f32[48,128]{1,0:T(8,128)S(1)} %bitcast.21), channel_id=1, source_target_pairs={{0,0},{1,32},{2,64},{3,96},{4,128},{5,160},{6,192},{7,224},{8,256}... | collective-permute-start | bytes 73736 | tf_op jit(solution)/shard_map/ppermute | solution.py:332
  11.8 30.0 %all_gather.17.g_ref = f32[1536,128]{1,0:T(8,128)S(1)} all-gather(f32[96,128]{1,0:T(8,128)S(1)} %all-gather), channel_id=1, replica_groups=mesh['row'=16,'xh'=2,'z'=16] {'z'}, dimensions={0}, use_global_device_ids=true | all-gather | bytes 835584 | tf_op jit(solution)/shard_map/all_gather | solution.py:333
  41.7 0.0 collective-permute-done.own_ref
  41.7 3.1 %shard_map.38 = (f32[1664,128]{1,0:T(8,128)S(1)}, f32[1024,128]{1,0:T(8,128)S(1)}, f32[1024,128]{1,0:T(8,128)S(1)}) custom-call(f32[4096,128]{1,0:T(8,128)} %bitcast.18, f32[1536,128]{1,0:T(8,128)S(1)} %all_gather.17.g_ref, f32[48,128]{1,0:T(8,128)S(1)} %collective-permute-done.own_ref), custom_call_target="tpu_custom_call" | custom-call | flops 201326592 | bytes 4808704 | tf_op jit(solution)/shard_map/pallas_call | solution.py:73
  44.9 30.0 %all_to_all.15 = f32[16,104,128]{2,1,0:T(8,128)S(1)} all-to-all(f32[16,104,128]{2,1,0:T(8,128)S(1)} %bitcast.16), channel_id=1, replica_groups=mesh['row'=16,'xh'=2,'z'=16] {'row'}, dimensions={0} | all-to-all | bytes 1703936 | tf_op jit(solution)/shard_map/all_to_all | solution.py:319
  74.9 1.8 %shard_map.39 = (f32[64,128]{1,0:T(8,128)S(1)}, f32[16,56,128]{2,1,0:T(8,128)}, f32[512,128]{1,0:T(8,128)}, f32[512,128]{1,0:T(8,128)}) custom-call(f32[1664,128]{1,0:T(8,128)S(1)} %bitcast.13), custom_call_target="tpu_custom_call" | custom-call | flops 18874368 | bytes 1867776 | tf_op jit(solution)/shard_map/pallas_call | solution.py:73
  76.6 4.5 %all-to-all-start.1 = ((f32[16,56,128]{2,1,0:T(8,128)}), f32[16,56,128]{2,1,0:T(8,128)S(1)}, u32[]{:S(2)}, u32[]{:S(2)}) async-start(f32[16,56,128]{2,1,0:T(8,128)} %get-tuple-element.23), calls=%async_computation.1 | async-start | bytes 917504 | tf_op jit(solution)/shard_map/all_to_all | solution.py:319
  81.2 0.0 copy-start
  81.2 23.5 %all-gather.1 = f32[1024,128]{1,0:T(8,128)S(1)} all-gather(f32[64,128]{1,0:T(8,128)S(1)} %get-tuple-element.30), channel_id=3, replica_groups=mesh['row'=16,'xh'=2,'z'=16] {'z'}, dimensions={0}, use_global_device_ids=true | all-gather | bytes 557056 | tf_op jit(solution)/shard_map/all_gather | solution.py:354
  104.7 1.1 shard_map.41
  105.7 0.0 all-to-all-done.1
  105.7 14.0 %all-to-all-start.2 = ((f32[32,64,128]{2,1,0:T(8,128)}), f32[32,64,128]{2,1,0:T(8,128)S(1)}, u32[]{:S(2)}, u32[]{:S(2)}) async-start(f32[32,64,128]{2,1,0:T(8,128)} %shard_map.41), calls=%async_computation.2 | async-start | bytes 2097152 | tf_op jit(solution)/shard_map/all_to_all | solution.py:319
  119.7 0.0 copy-done
  119.7 2.8 %shard_map.40 = (f32[192,512]{1,0:T(8,128)}, f32[192,512]{1,0:T(8,128)}, bf16[192,512]{1,0:T(8,128)(2,1)}, bf16[192,512]{1,0:T(8,128)(2,1)}, f32[96,96]{1,0:T(8,128)S(1)}, /*index=5*/f32[96,96]{1,0:T(8,128)S(1)}) custom-call(f32[512,128]{1,0:T(8,128)} %get-tuple-element.21.from_a, f32[512,128]{1,0:T(8,128)} %get-tuple-element.22.from_b, ...), custom_call_target="tpu_custom_call" | custom-call | flops 226492416 | bytes 2703360 | tf_op jit(solution)/shard_map/pallas_call | solution.py:73
  122.6 14.1 %all-to-all-done.2 = f32[32,64,128]{2,1,0:T(8,128)S(1)} async-done(((f32[32,64,128]{2,1,0:T(8,128)}), f32[32,64,128]{2,1,0:T(8,128)S(1)}, u32[]{:S(2)}, u32[]{:S(2)}) %all-to-all-start.2) | async-done | bytes 1048608 | tf_op jit(solution)/shard_map/all_to_all | solution.py:319
  136.7 5.5 %shard_map.42 = f32[4096,128]{1,0:T(8,128)} custom-call(f32[4096,128]{1,0:T(8,128)} %bitcast.19, f32[1024,128]{1,0:T(8,128)S(1)} %get-tuple-element.18.vra_ref, f32[1024,128]{1,0:T(8,128)S(1)} %get-tuple-element.19.vrb_ref, f32[192,512]{1,0:T(8,128)} %get-tuple-element.24.from_1, f32[192,512]{1,0:T(8,128)} %get-tuple-element.25.from_2, ...), custom_call_target="tpu_custom_call" | custom-call | flops 402653184 | bytes 8011776 | tf_op jit(solution)/shard_map/pallas_call | solution.py:73
  (1 shorter events, 0.0 us)
Async XLA Ops:
  0.0 0.8 copy-start.1
  6.3 35.5 %collective-permute-start = (f32[48,128]{1,0:T(8,128)S(1)}, f32[48,128]{1,0:T(8,128)S(1)}, u32[]{:S(2)}, u32[]{:S(2)}) collective-permute-start(f32[48,128]{1,0:T(8,128)S(1)} %bitcast.21), channel_id=1, source_target_pairs={{0,0},{1,32},{2,64},{3,96},{4,128},{5,160},{6,192},{7,224},{8,256}... | collective-permute-start | bytes 73736 | tf_op jit(solution)/shard_map/ppermute | solution.py:332
  76.6 29.1 %all-to-all-start.1 = ((f32[16,56,128]{2,1,0:T(8,128)}), f32[16,56,128]{2,1,0:T(8,128)S(1)}, u32[]{:S(2)}, u32[]{:S(2)}) async-start(f32[16,56,128]{2,1,0:T(8,128)} %get-tuple-element.23), calls=%async_computation.1 | async-start | bytes 917504 | tf_op jit(solution)/shard_map/all_to_all | solution.py:319
  81.2 38.6 %copy-start = (f32[2,96,96]{2,1,0:T(8,128)S(1)}, f32[2,96,96]{2,1,0:T(8,128)}, u32[]{:S(2)}) copy-start(f32[2,96,96]{2,1,0:T(8,128)} %t_ref.3) | copy-start | bytes 221188
  105.7 30.9 %all-to-all-start.2 = ((f32[32,64,128]{2,1,0:T(8,128)}), f32[32,64,128]{2,1,0:T(8,128)S(1)}, u32[]{:S(2)}, u32[]{:S(2)}) async-start(f32[32,64,128]{2,1,0:T(8,128)} %shard_map.41), calls=%async_computation.2 | async-start | bytes 2097152 | tf_op jit(solution)/shard_map/all_to_all | solution.py:319

commit v6 on v4

--- a/solution.py
+++ b/solution.py
@@ -188,7 +188,8 @@
         return here + r_ref[pl.ds(start + BLOCK, 16, stride=2 * BLOCK), :]
 
     def mul(a, b):
-        return plain(left_parts(a), right_parts(b))
+        (a1, a2), (b1, b2) = parts(a), parts(b)
+        return plain(a1, b1) + plain(a2, b1) + plain(a1, b2)
 
     wide = jnp.concatenate([both(48 + k) for k in range(6)], axis=0)
     low = jnp.concatenate([both(54 + k) for k in range(6)], axis=0)
@@ -239,14 +240,15 @@
             ]
     for i in range(4):
         at = slice(i * 256, i * 256 + 256)
+        y = yr_ref[:, at].T
         rows = jnp.concatenate(
-            [vra_ref[at, :], vrb_ref[at, :64], yr_ref[:, at].T], axis=1
+            [vra_ref[at, :], y[:, :128], vrb_ref[at, :64], y[:, 128:]], axis=1
         )
         left_ref[at, :] = left_parts(rows)
     vc = jnp.concatenate([vca_ref[...], vcb_ref[:, :64]], axis=1).T
     m1 = mul(left.T, yc_ref[...]) - mul(sym, vc)
     m2 = mul(left, vc)
-    right = right_parts(jnp.concatenate([m1, m2], axis=0))
+    right = right_parts(jnp.concatenate([m1[:128], m2[:128], m1[128:], m2[128:]], axis=0))
     for copy in copies:
         copy.wait()
     outs = []

time: 142 us -> 141 us (level)
  no operation moved by 1% of the time
where the time goes in v6:
time: 141 us; the launch traced here: 140 us
  blocking collectives  120 us (85%)
  starting transfers between devices  10 us (7%)
  Pallas kernels  9.84 us (7%)
    all_to_all x2, blocking collectives, spread(): return lax.all_to_all(array, axes, split_axis=0, concat_axis=0, tiled=True)  60.7 us
    all_gather x1, blocking collectives, shards(): lax.all_gather(pair.reshape(2 * SLICE, LANES), 'z', axis=0, tiled=True)  30 us
    all_gather x1, blocking collectives, shards(): block = lax.all_gather(block, 'z')  23.5 us
    pallas_call x5, Pallas kernels, call(): pl.pallas_call(kernel, out_shape=shapes, in_specs=[HBM if k in in_hbm els...  9.84 us
    ppermute x1, starting transfers between devices, shards(): own = lax.ppermute(own.reshape(SLICE, LANES), whole, same)  5.49 us
    all_gather x1, blocking collectives, shards(): pair = lax.all_gather(packed, 'xh')  5.44 us
    all_to_all x1, starting transfers between devices, spread(): return lax.all_to_all(array, axes, split_axis=0, concat_axis=0, tiled=True)  4.52 us
  transfers between devices with their start and end apart: 2, of which 0 were waited for; matrix products, arithmetic and copies ran while one was open for 0% of the time, Pallas kernels for 0%

profile of v6, /device:TPU:1, one launch (start us, length us, event | category | flops | bytes accessed | tf_op | source)
XLA Modules:
  0.0 140.3 jit_solution(8253178717019935648)
XLA Ops:
  0.0 0.0 copy-start.1
  0.0 0.8 copy-done.1
  0.8 0.1 shard_map.37
  0.8 5.4 %all-gather = f32[96,128]{1,0:T(8,128)S(1)} all-gather(f32[48,128]{1,0:T(8,128)S(1)} %shard_map.37), channel_id=2, replica_groups=mesh['row'=16,'xh'=2,'z'=16] {'xh'}, dimensions={0}, use_global_device_ids=true | all-gather | bytes 73728 | tf_op jit(solution)/shard_map/all_gather | solution.py:280
  6.3 5.5 %collective-permute-start = (f32[48,128]{1,0:T(8,128)S(1)}, f32[48,128]{1,0:T(8,128)S(1)}, u32[]{:S(2)}, u32[]{:S(2)}) collective-permute-start(f32[48,128]{1,0:T(8,128)S(1)} %bitcast.21), channel_id=1, source_target_pairs={{0,0},{1,32},{2,64},{3,96},{4,128},{5,160},{6,192},{7,224},{8,256}... | collective-permute-start | bytes 73736 | tf_op jit(solution)/shard_map/ppermute | solution.py:282
  11.8 30.0 %all_gather.17.g_ref = f32[1536,128]{1,0:T(8,128)S(1)} all-gather(f32[96,128]{1,0:T(8,128)S(1)} %all-gather), channel_id=1, replica_groups=mesh['row'=16,'xh'=2,'z'=16] {'z'}, dimensions={0}, use_global_device_ids=true | all-gather | bytes 835584 | tf_op jit(solution)/shard_map/all_gather | solution.py:283
  41.7 0.0 collective-permute-done.own_ref
  41.7 3.1 %shard_map.38 = (f32[1664,128]{1,0:T(8,128)S(1)}, f32[1024,128]{1,0:T(8,128)S(1)}, f32[1024,128]{1,0:T(8,128)S(1)}) custom-call(f32[4096,128]{1,0:T(8,128)} %bitcast.18, f32[1536,128]{1,0:T(8,128)S(1)} %all_gather.17.g_ref, f32[48,128]{1,0:T(8,128)S(1)} %collective-permute-done.own_ref), custom_call_target="tpu_custom_call" | custom-call | flops 201326592 | bytes 4808704 | tf_op jit(solution)/shard_map/pallas_call | solution.py:59
  44.9 30.0 %all_to_all.15 = f32[16,104,128]{2,1,0:T(8,128)S(1)} all-to-all(f32[16,104,128]{2,1,0:T(8,128)S(1)} %bitcast.16), channel_id=1, replica_groups=mesh['row'=16,'xh'=2,'z'=16] {'row'}, dimensions={0} | all-to-all | bytes 1703936 | tf_op jit(solution)/shard_map/all_to_all | solution.py:269
  74.9 1.2 shard_map.39
  76.0 4.5 %all-to-all-start.1 = ((f32[16,56,128]{2,1,0:T(8,128)}), f32[16,56,128]{2,1,0:T(8,128)S(1)}, u32[]{:S(2)}, u32[]{:S(2)}) async-start(f32[16,56,128]{2,1,0:T(8,128)} %get-tuple-element.17), calls=%async_computation.1 | async-start | bytes 917504 | tf_op jit(solution)/shard_map/all_to_all | solution.py:269
  80.5 0.0 copy-start
  80.5 23.5 %all-gather.1 = f32[1024,128]{1,0:T(8,128)S(1)} all-gather(f32[64,128]{1,0:T(8,128)S(1)} %get-tuple-element.18), channel_id=3, replica_groups=mesh['row'=16,'xh'=2,'z'=16] {'z'}, dimensions={0}, use_global_device_ids=true | all-gather | bytes 557056 | tf_op jit(solution)/shard_map/all_gather | solution.py:303
  104.1 0.1 shard_map.40
  104.1 0.0 all-to-all-done.1
  104.1 30.7 %all_to_all.16 = f32[32,64,128]{2,1,0:T(8,128)S(1)} all-to-all(f32[32,64,128]{2,1,0:T(8,128)S(1)} %shard_map.40), channel_id=1, replica_groups=mesh['row'=16,'xh'=2,'z'=16] {'row','xh'}, dimensions={0} | all-to-all | bytes 2097152 | tf_op jit(solution)/shard_map/all_to_all | solution.py:269
  134.9 0.0 copy-done
  134.9 5.4 %shard_map.41 = f32[4096,128]{1,0:T(8,128)} custom-call(f32[4096,128]{1,0:T(8,128)} %bitcast.19, f32[1024,128]{1,0:T(8,128)S(1)} %get-tuple-element.12.vra_ref, f32[1024,128]{1,0:T(8,128)S(1)} %get-tuple-element.13.vrb_ref, f32[512,128]{1,0:T(8,128)S(1)} %get-tuple-element.15.vca_ref, f32[512,128]{1,0:T(8,128)S(1)} %get-tuple-element.16.vcb_ref, ...), custom_call_target="tpu_custom_call" | custom-call | flops 402653184 | bytes 7348224 | tf_op jit(solution)/shard_map/pallas_call | solution.py:59
  (1 shorter events, 0.0 us)
Async XLA Ops:
  0.0 0.8 copy-start.1
  6.3 35.5 %collective-permute-start = (f32[48,128]{1,0:T(8,128)S(1)}, f32[48,128]{1,0:T(8,128)S(1)}, u32[]{:S(2)}, u32[]{:S(2)}) collective-permute-start(f32[48,128]{1,0:T(8,128)S(1)} %bitcast.21), channel_id=1, source_target_pairs={{0,0},{1,32},{2,64},{3,96},{4,128},{5,160},{6,192},{7,224},{8,256}... | collective-permute-start | bytes 73736 | tf_op jit(solution)/shard_map/ppermute | solution.py:282
  76.0 28.1 %all-to-all-start.1 = ((f32[16,56,128]{2,1,0:T(8,128)}), f32[16,56,128]{2,1,0:T(8,128)S(1)}, u32[]{:S(2)}, u32[]{:S(2)}) async-start(f32[16,56,128]{2,1,0:T(8,128)} %get-tuple-element.17), calls=%async_computation.1 | async-start | bytes 917504 | tf_op jit(solution)/shard_map/all_to_all | solution.py:269
  80.5 54.3 %copy-start = (f32[2,96,96]{2,1,0:T(8,128)S(1)}, f32[2,96,96]{2,1,0:T(8,128)}, u32[]{:S(2)}) copy-start(f32[2,96,96]{2,1,0:T(8,128)} %t_ref.1) | copy-start | bytes 221188

commit v7 on v6

--- a/solution.py
+++ b/solution.py
@@ -90,7 +90,7 @@
 
 
 def image_kernel(hbm_ref, g_ref, own_ref, send_ref, va_ref, vb_ref, a_ref, sem):
-    copies = fetch(hbm_ref, a_ref, sem, 8)
+    copies = fetch(hbm_ref, a_ref, sem, 4)
     for x in range(XS):
         for j in range(4):
             for h in range(2):
@@ -115,8 +115,7 @@
         v = jnp.concatenate([va_ref[at, :], vb_ref[at, :64]], axis=1)
         left = left_parts(v.T)
         gram = gram + plain(left[:W], right_parts(v[:, W:]))
-        copies[2 * c].wait()
-        copies[2 * c + 1].wait()
+        copies[c].wait()
         tiles = [a_ref[pl.ds(c * 1024 + j, 256, stride=4), :] for j in range(4)]
         q = q + plain(left, right_parts(jnp.concatenate(tiles, axis=1)))
     for j in range(4):
@@ -187,9 +186,11 @@
         here = r_ref[pl.ds(start, 16, stride=2 * BLOCK), :]
         return here + r_ref[pl.ds(start + BLOCK, 16, stride=2 * BLOCK), :]
 
+    def times(a, b):
+        return plain(a[0], b[0]) + plain(a[1], b[0]) + plain(a[0], b[1])
+
     def mul(a, b):
-        (a1, a2), (b1, b2) = parts(a), parts(b)
-        return plain(a1, b1) + plain(a2, b1) + plain(a1, b2)
+        return times(parts(a), parts(b))
 
     wide = jnp.concatenate([both(48 + k) for k in range(6)], axis=0)
     low = jnp.concatenate([both(54 + k) for k in range(6)], axis=0)
@@ -245,9 +246,9 @@
             [vra_ref[at, :], y[:, :128], vrb_ref[at, :64], y[:, 128:]], axis=1
         )
         left_ref[at, :] = left_parts(rows)
-    vc = jnp.concatenate([vca_ref[...], vcb_ref[:, :64]], axis=1).T
-    m1 = mul(left.T, yc_ref[...]) - mul(sym, vc)
-    m2 = mul(left, vc)
+    vc = parts(jnp.concatenate([vca_ref[...], vcb_ref[:, :64]], axis=1).T)
+    m1 = mul(left.T, yc_ref[...]) - times(parts(sym), vc)
+    m2 = times(parts(left), vc)
     right = right_parts(jnp.concatenate([m1[:128], m2[:128], m1[128:], m2[128:]], axis=0))
     for copy in copies:
         copy.wait()
@@ -284,7 +285,7 @@
     image, vra, vrb = call(
         image_kernel,
         [(ROWS * SEND, LANES), (1024, LANES), (1024, LANES)],
-        [(4096, LANES), pltpu.SemaphoreType.DMA((8,))],
+        [(4096, LANES), pltpu.SemaphoreType.DMA((4,))],
         2 * 1024 * 512 * 192,
         blocks,
         gathered,

time: 141 us -> 141 us (level)
  no operation moved by 1% of the time
where the time goes in v7:
time: 141 us; the launch traced here: 140 us
  blocking collectives  120 us (85%)
  starting transfers between devices  10 us (7%)
  Pallas kernels  9.79 us (7%)
    all_to_all x2, blocking collectives, spread(): return lax.all_to_all(array, axes, split_axis=0, concat_axis=0, tiled=True)  60.7 us
    all_gather x1, blocking collectives, shards(): lax.all_gather(pair.reshape(2 * SLICE, LANES), 'z', axis=0, tiled=True)  30 us
    all_gather x1, blocking collectives, shards(): block = lax.all_gather(block, 'z')  23.5 us
    pallas_call x5, Pallas kernels, call(): pl.pallas_call(kernel, out_shape=shapes, in_specs=[HBM if k in in_hbm els...  9.79 us
    ppermute x1, starting transfers between devices, shards(): own = lax.ppermute(own.reshape(SLICE, LANES), whole, same)  5.49 us
    all_gather x1, blocking collectives, shards(): pair = lax.all_gather(packed, 'xh')  5.44 us
    all_to_all x1, starting transfers between devices, spread(): return lax.all_to_all(array, axes, split_axis=0, concat_axis=0, tiled=True)  4.52 us
  transfers between devices with their start and end apart: 2, of which 0 were waited for; matrix products, arithmetic and copies ran while one was open for 0% of the time, Pallas kernels for 0%

profile of v7, /device:TPU:1, one launch (start us, length us, event | category | flops | bytes accessed | tf_op | source)
XLA Modules:
  0.0 140.2 jit_solution(10407002950712062308)
XLA Ops:
  0.0 0.0 copy-start.1
  0.0 0.8 copy-done.1
  0.8 0.1 shard_map.37
  0.8 5.4 %all-gather = f32[96,128]{1,0:T(8,128)S(1)} all-gather(f32[48,128]{1,0:T(8,128)S(1)} %shard_map.37), channel_id=2, replica_groups=mesh['row'=16,'xh'=2,'z'=16] {'xh'}, dimensions={0}, use_global_device_ids=true | all-gather | bytes 73728 | tf_op jit(solution)/shard_map/all_gather | solution.py:281
  6.3 5.5 %collective-permute-start = (f32[48,128]{1,0:T(8,128)S(1)}, f32[48,128]{1,0:T(8,128)S(1)}, u32[]{:S(2)}, u32[]{:S(2)}) collective-permute-start(f32[48,128]{1,0:T(8,128)S(1)} %bitcast.21), channel_id=1, source_target_pairs={{0,0},{1,32},{2,64},{3,96},{4,128},{5,160},{6,192},{7,224},{8,256}... | collective-permute-start | bytes 73736 | tf_op jit(solution)/shard_map/ppermute | solution.py:283
  11.8 30.0 %all_gather.17.g_ref = f32[1536,128]{1,0:T(8,128)S(1)} all-gather(f32[96,128]{1,0:T(8,128)S(1)} %all-gather), channel_id=1, replica_groups=mesh['row'=16,'xh'=2,'z'=16] {'z'}, dimensions={0}, use_global_device_ids=true | all-gather | bytes 835584 | tf_op jit(solution)/shard_map/all_gather | solution.py:284
  41.7 0.0 collective-permute-done.own_ref
  41.7 3.1 %shard_map.38 = (f32[1664,128]{1,0:T(8,128)S(1)}, f32[1024,128]{1,0:T(8,128)S(1)}, f32[1024,128]{1,0:T(8,128)S(1)}) custom-call(f32[4096,128]{1,0:T(8,128)} %bitcast.18, f32[1536,128]{1,0:T(8,128)S(1)} %all_gather.17.g_ref, f32[48,128]{1,0:T(8,128)S(1)} %collective-permute-done.own_ref), custom_call_target="tpu_custom_call" | custom-call | flops 201326592 | bytes 4808704 | tf_op jit(solution)/shard_map/pallas_call | solution.py:59
  44.8 30.0 %all_to_all.15 = f32[16,104,128]{2,1,0:T(8,128)S(1)} all-to-all(f32[16,104,128]{2,1,0:T(8,128)S(1)} %bitcast.16), channel_id=1, replica_groups=mesh['row'=16,'xh'=2,'z'=16] {'row'}, dimensions={0} | all-to-all | bytes 1703936 | tf_op jit(solution)/shard_map/all_to_all | solution.py:270
  74.8 1.2 shard_map.39
  76.0 4.5 %all-to-all-start.1 = ((f32[16,56,128]{2,1,0:T(8,128)}), f32[16,56,128]{2,1,0:T(8,128)S(1)}, u32[]{:S(2)}, u32[]{:S(2)}) async-start(f32[16,56,128]{2,1,0:T(8,128)} %get-tuple-element.17), calls=%async_computation.1 | async-start | bytes 917504 | tf_op jit(solution)/shard_map/all_to_all | solution.py:270
  80.5 0.0 copy-start
  80.5 23.5 %all-gather.1 = f32[1024,128]{1,0:T(8,128)S(1)} all-gather(f32[64,128]{1,0:T(8,128)S(1)} %get-tuple-element.18), channel_id=3, replica_groups=mesh['row'=16,'xh'=2,'z'=16] {'z'}, dimensions={0}, use_global_device_ids=true | all-gather | bytes 557056 | tf_op jit(solution)/shard_map/all_gather | solution.py:304
  104.0 0.1 shard_map.40
  104.1 0.0 all-to-all-done.1
  104.1 30.7 %all_to_all.16 = f32[32,64,128]{2,1,0:T(8,128)S(1)} all-to-all(f32[32,64,128]{2,1,0:T(8,128)S(1)} %shard_map.40), channel_id=1, replica_groups=mesh['row'=16,'xh'=2,'z'=16] {'row','xh'}, dimensions={0} | all-to-all | bytes 2097152 | tf_op jit(solution)/shard_map/all_to_all | solution.py:270
  134.8 0.0 copy-done
  134.8 5.4 %shard_map.41 = f32[4096,128]{1,0:T(8,128)} custom-call(f32[4096,128]{1,0:T(8,128)} %bitcast.19, f32[1024,128]{1,0:T(8,128)S(1)} %get-tuple-element.12.vra_ref, f32[1024,128]{1,0:T(8,128)S(1)} %get-tuple-element.13.vrb_ref, f32[512,128]{1,0:T(8,128)S(1)} %get-tuple-element.15.vca_ref, f32[512,128]{1,0:T(8,128)S(1)} %get-tuple-element.16.vcb_ref, ...), custom_call_target="tpu_custom_call" | custom-call | flops 402653184 | bytes 7348224 | tf_op jit(solution)/shard_map/pallas_call | solution.py:59
  (1 shorter events, 0.0 us)
Async XLA Ops:
  0.0 0.8 copy-start.1
  6.3 35.5 %collective-permute-start = (f32[48,128]{1,0:T(8,128)S(1)}, f32[48,128]{1,0:T(8,128)S(1)}, u32[]{:S(2)}, u32[]{:S(2)}) collective-permute-start(f32[48,128]{1,0:T(8,128)S(1)} %bitcast.21), channel_id=1, source_target_pairs={{0,0},{1,32},{2,64},{3,96},{4,128},{5,160},{6,192},{7,224},{8,256}... | collective-permute-start | bytes 73736 | tf_op jit(solution)/shard_map/ppermute | solution.py:283
  76.0 28.1 %all-to-all-start.1 = ((f32[16,56,128]{2,1,0:T(8,128)}), f32[16,56,128]{2,1,0:T(8,128)S(1)}, u32[]{:S(2)}, u32[]{:S(2)}) async-start(f32[16,56,128]{2,1,0:T(8,128)} %get-tuple-element.17), calls=%async_computation.1 | async-start | bytes 917504 | tf_op jit(solution)/shard_map/all_to_all | solution.py:270
  80.5 54.3 %copy-start = (f32[2,96,96]{2,1,0:T(8,128)S(1)}, f32[2,96,96]{2,1,0:T(8,128)}, u32[]{:S(2)}) copy-start(f32[2,96,96]{2,1,0:T(8,128)} %t_ref.1) | copy-start | bytes 221188
